TPU v7x, 128 devices: a whole 4x4x4 slice. The times are simulated.
128 devices in a mesh: row: 8 (over y, z_lo), col: 16 (over x, z_hi, core).
Axes of the slice: x: 4, y: 4, z: 4 (z_hi: 2, z_lo: 2; z = z_hi * 2 + z_lo), core: 2. Of those that a mesh axis runs over, the one named last changes fastest.
Arguments:
- tokens: bfloat16 [1024, 12288], P('col', 'row'), may hold values from -1.5 to 1.5
- weight: bfloat16 [12288, 49152], P('row', 'col'), may hold values from -0.0546875 to 0.0546875
- pre_act: bfloat16 [1024, 49152], P('row', 'col'), may hold values from -6 to 6
- upstream: bfloat16 [1024, 49152], P('row', 'col'), may hold values from -6 to 6
Outputs:
- input_grad: bfloat16 [1024, 12288], P('col', 'row')
- weight_grad: bfloat16 [12288, 49152], P('row', 'col')
All inputs are finite; a program needn't handle non-finite values.
Results may differ from a plain program's by a relative error of at most 0.0049.
Values may be sent and summed in bfloat16 or wider, within the bound.
No kernel may reach another device: no remote copies, remote signals or barrier semaphores. Data moves between devices by JAX's collectives and lax.ppermute only.
A program may use at most 128 MiB of HBM per device.

v0:
```python
import math

import jax
import jax.numpy as jnp
from jax import lax
from jax.sharding import PartitionSpec as P


def gelu_slope(value):
    scale = math.sqrt(2.0 / math.pi)
    inner = scale * (value + 0.044715 * value * value * value)
    tangent = jnp.tanh(inner)
    return 0.5 * (1.0 + tangent) + 0.5 * value * (1.0 - tangent * tangent) * scale * (
        1.0 + 3.0 * 0.044715 * value * value
    )


def hidden_gradient(pre_values, up_values):
    return (up_values.astype(jnp.float32) * gelu_slope(pre_values.astype(jnp.float32))).astype(
        jnp.bfloat16
    )


def local(tokens, weight, pre_act, upstream):
    grad_local = hidden_gradient(pre_act, upstream)
    grad_all = lax.all_gather(grad_local, "row", axis=0, tiled=True)
    token_all = lax.all_gather(tokens, "col", axis=0, tiled=True)
    weight_grad = lax.dot_general(
        token_all, grad_all, (((0,), (0,)), ((), ())), preferred_element_type=jnp.float32
    ).astype(jnp.bfloat16)
    partial_sums = lax.dot_general(
        grad_all, weight, (((1,), (1,)), ((), ())), preferred_element_type=jnp.float32
    )
    input_grad = lax.psum_scatter(partial_sums, "col", scatter_dimension=0, tiled=True).astype(
        jnp.bfloat16
    )
    return (input_grad, weight_grad)


def solution(mesh):
    in_specs = (P("col", "row"), P("row", "col"), P("row", "col"), P("row", "col"))
    out_specs = (P("col", "row"), P("row", "col"))
    return jax.shard_map(local, mesh=mesh, in_specs=in_specs, out_specs=out_specs, check_vma=False)
```

profile of v0, /device:TPU:0, one launch (start us, length us, event | category | flops | bytes accessed | tf_op | source)
XLA Modules:
  0.0 299.1 jit_solution(7833875887188668540)
XLA Ops:
  7.2 0.0 all-gather.3.cloned.1.call-start
  7.2 3.3 %fusion.8 = bf16[128,3072]{1,0:T(8,128)(2,1)} fusion(bf16[128,3072]{1,0:T(8,128)(2,1)} %param.6, bf16[128,3072]{1,0:T(8,128)(2,1)} %param.7), kind=kLoop, calls=%fused_computation.16 | loop fusion | flops 8257536 | bytes 2359296 | tf_op jit(solution)/shard_map/convert_element_type | solution.py:19
  10.6 0.0 all-gather.3.cloned.1.call-update
  10.6 0.0 all-gather.5.cloned.1.call-start
  10.6 0.7 all-gather.5.cloned.1.call-update
  11.3 0.0 reduce-scatter.2.cloned.1.call-start
  11.4 130.9 %all-gather.3.cloned.1.call-done = bf16[1024,3072]{1,0:T(8,128)(2,1)} async-done(((bf16[128,3072]{1,0:T(8,128)(2,1)}), bf16[1024,3072]{1,0:T(8,128)(2,1)}) %all-gather.3.cloned.1.call-update) | async-done | bytes 6291472 | tf_op jit(solution)/shard_map/all_gather | solution.py:26
  142.3 15.6 %fusion.10 = f32[1024,1536]{1,0:T(8,128)} fusion(bf16[1024,3072]{1,0:T(8,128)(2,1)} %all-gather.3.cloned.1.call-done, bf16[1536,3072]{1,0:T(8,128)(2,1)} %param.5), kind=kOutput, calls=%fused_computation.18 | convolution fusion | flops 9663676416 | bytes 22020096 | tf_op jit(solution)/shard_map/dot_general | solution.py:31
  157.8 0.0 reduce-scatter.2.cloned.1.call-update
  157.9 40.6 %all-gather.5.cloned.1.call-done = bf16[1024,1536]{1,0:T(8,128)(2,1)} async-done(((bf16[64,1536]{1,0:T(8,128)(2,1)}), bf16[1024,1536]{1,0:T(8,128)(2,1)}) %all-gather.5.cloned.1.call-update) | async-done | bytes 3145744 | tf_op jit(solution)/shard_map/all_gather | solution.py:27
  198.4 15.2 %fusion = bf16[1536,3072]{0,1:T(8,128)(2,1)} fusion(bf16[1024,3072]{1,0:T(8,128)(2,1)} %all-gather.3.cloned.1.call-done, bf16[1024,1536]{1,0:T(8,128)(2,1)} %all-gather.5.cloned.1.call-done), kind=kOutput, calls=%fused_computation.1 | convolution fusion | flops 9668395008 | bytes 18874368 | tf_op jit(solution)/shard_map/dot_general | solution.py:28
  213.7 13.0 %copy.6 = bf16[1536,3072]{1,0:T(8,128)(2,1)} copy(bf16[1536,3072]{0,1:T(8,128)(2,1)} %fusion) | data formatting | bytes 18874368
  226.7 64.3 %reduce-scatter.2.cloned.1.call-done = f32[64,1536]{1,0:T(8,128)} async-done(((f32[1024,1536]{1,0:T(8,128)}), f32[64,1536]{1,0:T(8,128)}) %reduce-scatter.2.cloned.1.call-update) | async-done | bytes 393232 | tf_op jit(solution)/shard_map/reduce_scatter | solution.py:34
  290.9 1.7 convert_element_type.21
Async XLA Ops:
  7.2 135.1 %all-gather.3.cloned.1.call-start = ((), (), s32[]{:S(2)}) async-start(), calls=%async_computation.1 | async-start | bytes 7077888 | tf_op jit(solution)/shard_map/all_gather | solution.py:26
  10.6 187.9 %all-gather.5.cloned.1.call-start = ((), (), s32[]{:S(2)}) async-start(), calls=%async_computation.3 | async-start | bytes 3342336 | tf_op jit(solution)/shard_map/all_gather | solution.py:27
  11.3 279.6 %reduce-scatter.2.cloned.1.call-start = ((), (), s32[]{:S(2)}) async-start(), calls=%async_computation.2 | async-start | bytes 6684672 | tf_op jit(solution)/shard_map/reduce_scatter | solution.py:34
Sparse Core Ops, SparseCore 0:
  10.7 131.5 all-gather.2
  144.7 53.7 all-gather.4
  202.6 88.2 reduce-scatter.1
where the time goes:
time: 300 us; the launch traced here: 299 us
  waiting for transfers between devices  236 us (79%)
  matrix products  30.8 us (10%)
  between operations  13.7 us (5%)
  local copies, waits for them, and re-layouts  13 us (4%)
  other arithmetic  5.04 us (2%)
    all_gather x1, waiting for transfers between devices, local(): grad_all = lax.all_gather(grad_local, 'row', axis=0, tiled=True)  131 us
    reduce_scatter x1, waiting for transfers between devices, local(): lax.psum_scatter(partial_sums, 'col', scatter_dimension=0, tiled=True)  64.3 us
    all_gather x1, waiting for transfers between devices, local(): token_all = lax.all_gather(tokens, 'col', axis=0, tiled=True)  40.6 us
    dot_general x1, matrix products, local(): lax.dot_general(grad_all, weight, (((1,), (1,)), ((), ())), preferred_ele...  15.6 us
    dot_general x1, matrix products, local(): lax.dot_general(token_all, grad_all, (((0,), (0,)), ((), ())), preferred_...  15.2 us
    unnamed x1, local copies, waits for them, and re-layouts  13 us
  transfers between devices with their start and end apart: 3, of which 3 were waited for; matrix products, arithmetic and copies ran while one was open for 15% of the time, Pallas kernels for 0%

commit v1 on v0

v1 whole, which is shorter than its diff:
```python
import functools
import math

import jax
import jax.numpy as jnp
from jax import lax
from jax.experimental import pallas as pl
from jax.experimental.pallas import tpu as pltpu
from jax.sharding import PartitionSpec as P

BF, F32 = jnp.bfloat16, jnp.float32
LIMIT = 48 * 1024 * 1024


def params(limit=LIMIT):
    return pltpu.CompilerParams(vmem_limit_bytes=limit)


def cost(flops, bytes_accessed):
    return pl.CostEstimate(flops=flops, bytes_accessed=bytes_accessed, transcendentals=0)


def place():
    row, col = lax.axis_index("row"), lax.axis_index("col")
    return row // 2, row % 2, col // 4, (col // 2) % 2, col % 2


def row_shift(value, dy, dz=0):
    pairs = [(y * 2 + z, ((y + dy) % 4) * 2 + (z + dz) % 2) for y in range(4) for z in range(2)]
    return lax.ppermute(value, "row", pairs)


def col_shift(value, dx, dh=0, dk=0):
    pairs = [
        (x * 4 + h * 2 + k, ((x + dx) % 4) * 4 + ((h + dh) % 2) * 2 + (k + dk) % 2)
        for x in range(4)
        for h in range(2)
        for k in range(2)
    ]
    return lax.ppermute(value, "col", pairs)


def slope_kernel(pre_ref, up_ref, out_ref):
    value = pre_ref[...].astype(F32)
    scale = math.sqrt(2.0 / math.pi)
    square = value * value
    tangent = jnp.tanh(scale * (value + 0.044715 * value * square))
    slope = 0.5 * (1.0 + tangent) + 0.5 * value * (1.0 - tangent * tangent) * scale * (
        1.0 + 3.0 * 0.044715 * square
    )
    out_ref[...] = (up_ref[...].astype(F32) * slope).astype(BF)


def hidden_gradient(pre_act, upstream, start, width, step=512):
    rows = pre_act.shape[0]
    spec = pl.BlockSpec((rows, step), lambda j: (0, j + start // step))
    return pl.pallas_call(
        slope_kernel,
        out_shape=jax.ShapeDtypeStruct((rows, width), BF),
        grid=(width // step,),
        in_specs=[spec, spec],
        out_specs=pl.BlockSpec((rows, step), lambda j: (0, j)),
        compiler_params=params(),
        cost_estimate=cost(30 * rows * width, 6 * rows * width),
        name="hidden_gradient",
    )(pre_act, upstream)


def transpose_kernel(*refs):
    pieces, out_ref, whole, sem = refs[:8], refs[8], refs[9], refs[10]
    _, _, x, h, core = place()
    copies = []
    for number, piece in enumerate(pieces):
        shift, other = number % 4, number // 4
        owner = (x + 4 - shift) % 4
        side = (core + other) % 2
        for dh in range(2):
            offset = (owner * 2 + (h + dh) % 2) * 128 + side * 64
            copies.append(
                pltpu.make_async_copy(
                    piece.at[dh],
                    whole.at[pl.ds(pl.multiple_of(offset, 64), 64), :],
                    sem.at[number, dh],
                )
            )
    for copy in copies:
        copy.start()
    for copy in copies:
        copy.wait()
    width = whole.shape[1]
    for start in range(0, width, 256):
        out_ref[start : start + 256, :] = whole[:, start : start + 256].T


def transposed_tokens(pieces):
    width = pieces[0].shape[2]
    rows = 1024
    return pl.pallas_call(
        transpose_kernel,
        out_shape=jax.ShapeDtypeStruct((width, rows), BF),
        in_specs=[pl.BlockSpec(memory_space=pl.ANY)] * 8,
        out_specs=pl.BlockSpec(memory_space=pltpu.VMEM),
        scratch_shapes=[pltpu.VMEM((rows, width), BF), pltpu.SemaphoreType.DMA((8, 2))],
        compiler_params=params(),
        cost_estimate=cost(0, 8 * rows * width),
        name="transposed_tokens",
    )(*pieces)


def input_kernel(blocks, *refs):
    pieces, weight_ref = refs[: 2 * blocks], refs[2 * blocks]
    own_ref, send_ref, held, sem = refs[2 * blocks + 1 :]
    core = lax.axis_index("col") % 2
    rows = 128

    @pl.when(pl.program_id(0) == 0)
    def _():
        copies = []
        for number in range(blocks):
            at = 0
            for part in range(2):
                piece = pieces[2 * number + part]
                width = piece.shape[1]
                copies.append(
                    pltpu.make_async_copy(
                        piece,
                        held.at[pl.ds(number * rows, rows), pl.ds(at, width)],
                        sem.at[number, part],
                    )
                )
                at += width
        for copy in copies:
            copy.start()
        for copy in copies:
            copy.wait()

    total = lax.dot_general(
        held[...], weight_ref[...], (((1,), (1,)), ((), ())), preferred_element_type=F32
    )
    total = total.reshape(blocks, 2, 64, total.shape[1])

    @pl.when(core == 0)
    def _():
        own_ref[...] = total[:, 0]
        send_ref[...] = total[:, 1].astype(BF)

    @pl.when(core == 1)
    def _():
        own_ref[...] = total[:, 1]
        send_ref[...] = total[:, 0].astype(BF)


def input_part(blocks, weight, step=256):
    count = len(blocks)
    features, hidden = weight.shape
    pieces = [piece for block in blocks for piece in block]
    spec = pl.BlockSpec((count, 64, step), lambda j: (0, 0, j))
    return pl.pallas_call(
        functools.partial(input_kernel, count),
        out_shape=(
            jax.ShapeDtypeStruct((count, 64, features), F32),
            jax.ShapeDtypeStruct((count, 64, features), BF),
        ),
        grid=(features // step,),
        in_specs=[pl.BlockSpec(memory_space=pl.ANY)] * (2 * count)
        + [pl.BlockSpec((step, hidden), lambda j: (j, 0))],
        out_specs=(spec, spec),
        scratch_shapes=[
            pltpu.VMEM((count * 128, hidden), BF),
            pltpu.SemaphoreType.DMA((count, 2)),
        ],
        compiler_params=params(),
        cost_estimate=cost(
            2 * count * 128 * features * hidden, 2 * features * hidden + 2 * count * 128 * hidden
        ),
        name="input_part",
    )(*pieces, weight)


def deal_kernel(groups, *refs):
    ins, outs = refs[: 2 * len(groups)], refs[2 * len(groups) : 2 * len(groups) + 4]
    both = refs[-1]
    y, _, x, _, _ = place()
    for number, group in enumerate(groups):
        own, received = ins[2 * number], ins[2 * number + 1]
        for at, dy in enumerate(group):
            both[dy] = own[at] + received[at].astype(F32)
    for dx in range(4):
        outs[dx][...] = both[(x + dx + 4 - y) % 4].astype(outs[dx].dtype)


def dealt(groups, arrays):
    rows, features = arrays[0].shape[1:]
    return pl.pallas_call(
        functools.partial(deal_kernel, groups),
        out_shape=[jax.ShapeDtypeStruct((rows, features), F32)]
        + [jax.ShapeDtypeStruct((rows, features), BF)] * 3,
        in_specs=[pl.BlockSpec(memory_space=pltpu.VMEM)] * len(arrays),
        out_specs=[pl.BlockSpec(memory_space=pltpu.VMEM)] * 4,
        scratch_shapes=[pltpu.VMEM((4, rows, features), F32)],
        compiler_params=params(),
        cost_estimate=cost(0, 40 * rows * features),
        name="dealt",
    )(*arrays)


def weight_kernel(tile, *refs):
    pieces, token_ref, out_ref, held, sem = refs[:16], refs[16], refs[17], refs[18], refs[19]
    y, z, _, _, _ = place()
    tiles = held.shape[1] // tile
    j = pl.program_id(0)

    def copies(at):
        made = []
        for number in range(8):
            dy, dz = number % 4, number // 4
            owner = ((y + dy) % 4) * 2 + (z + dz) % 2
            start = at * tile
            piece, inside = pieces[2 * number], start
            if start >= piece.shape[1]:
                piece, inside = pieces[2 * number + 1], start - piece.shape[1]
            made.append(
                pltpu.make_async_copy(
                    piece.at[:, pl.ds(inside, tile)],
                    held.at[pl.ds(pl.multiple_of(owner * 128, 128), 128), pl.ds(start, tile)],
                    sem.at[number, at],
                )
            )
        return made

    @pl.when(j == 0)
    def _():
        for at in range(tiles):
            for copy in copies(at):
                copy.start()

    for at in range(tiles):

        @pl.when(j == at)
        def _(at=at):
            for copy in copies(at):
                copy.wait()
            out_ref[...] = jnp.dot(
                token_ref[...], held[:, at * tile : (at + 1) * tile], preferred_element_type=F32
            ).astype(BF)


def weight_gradient(tokens_t, blocks, hidden, tile=512):
    features, rows = tokens_t.shape
    pieces = [piece for block in blocks for piece in block]
    return pl.pallas_call(
        functools.partial(weight_kernel, tile),
        out_shape=jax.ShapeDtypeStruct((features, hidden), BF),
        grid=(hidden // tile,),
        in_specs=[pl.BlockSpec(memory_space=pl.ANY)] * 16
        + [pl.BlockSpec((features, rows), lambda j: (0, 0))],
        out_specs=pl.BlockSpec((features, tile), lambda j: (0, j)),
        scratch_shapes=[
            pltpu.VMEM((rows, hidden), BF),
            pltpu.SemaphoreType.DMA((8, hidden // tile)),
        ],
        compiler_params=params(),
        cost_estimate=cost(2 * rows * features * hidden, 2 * features * hidden),
        name="weight_gradient",
    )(*pieces, tokens_t)


def local(tokens, weight, pre_act, upstream):
    y, z, x, h, core = place()
    hidden = pre_act.shape[1]
    first = hidden * 2 // 3
    a = hidden_gradient(pre_act, upstream, 0, first)
    b = hidden_gradient(pre_act, upstream, first, hidden - first)

    za = row_shift(a, 0, 1)
    ua, da = row_shift(a, 1), row_shift(a, -1)
    zb = row_shift(b, 0, 1)
    ub, db = row_shift(b, 1), row_shift(b, -1)
    qa, qb = row_shift(ua, 1), row_shift(db, -1)
    zua, zda = row_shift(za, 1), row_shift(za, -1)
    zub, zdb = row_shift(ub, 0, 1), row_shift(db, 0, 1)
    zqa, zqb = row_shift(zda, -1), row_shift(qb, 0, 1)

    pair = jnp.stack([tokens, col_shift(tokens, 0, 1)])
    mine = [pair] + [col_shift(pair, dx) for dx in (1, 2, 3)]
    others = [col_shift(value, 0, 0, 1) for value in mine]
    tokens_t = transposed_tokens(mine + others)

    near = [(a, b), (da, db), (qa, qb), (ua, ub)]
    far = [(za, zb), (zda, zdb), (zqa, zqb), (zua, zub)]

    own1, send1 = input_part(near, weight)
    got1 = col_shift(send1, 0, 0, 1)
    s0, s1, s2, s3 = dealt(((0, 1, 2, 3),), [own1, got1])
    r1, r2, r3 = col_shift(s1, 1), col_shift(s2, 2), col_shift(s3, 3)
    sum1 = s0 + r1.astype(F32) + r2.astype(F32) + r3.astype(F32)

    own2, send2 = input_part([far[0], far[1], far[3]], weight)
    got2 = col_shift(send2, 0, 0, 1)
    own3, send3 = input_part([far[2]], weight)
    got3 = col_shift(send3, 0, 0, 1)
    t0, t1, t2, t3 = dealt(((0, 1, 3), (2,)), [own2, got2, own3, got3])
    v1, v2, v3 = col_shift(t1, 1), col_shift(t2, 2), col_shift(t3, 3)

    weight_grad = weight_gradient(tokens_t, near + far, hidden)

    sum2 = t0 + v1.astype(F32) + v2.astype(F32) + v3.astype(F32)
    owner = h == z
    last = col_shift(jnp.where(owner, sum2, sum1).astype(BF), 0, 1)
    input_grad = (jnp.where(owner, sum1, sum2) + last.astype(F32)).astype(BF)
    return (input_grad, weight_grad)


def solution(mesh):
    in_specs = (P("col", "row"), P("row", "col"), P("row", "col"), P("row", "col"))
    out_specs = (P("col", "row"), P("row", "col"))
    return jax.shard_map(local, mesh=mesh, in_specs=in_specs, out_specs=out_specs, check_vma=False)
```

time: 300 us -> 142 us (0.47)
  waiting for transfers between devices: 236 us -> 38.6 us
  Pallas kernels: 0 us -> 51.3 us
  starting transfers between devices: 0.12 us -> 36.8 us
  matrix products: 30.8 us -> 0 us
  between operations: 13.7 us -> 1.16 us
    all_gather x2 -> x0, waiting for transfers between devices: 171 us -> none  [the longest x1 131 us: local(): grad_all = lax.all_gather(grad_local, 'row', axis=0, tiled=True)]
    reduce_scatter x1 -> x0, waiting for transfers between devices: 64.3 us -> none  [local(): lax.psum_scatter(partial_sums, 'col', scatter_dimension=0, tiled=True)]
    pallas_call x0 -> x9, Pallas kernels: none -> 51.3 us  [the longest x3 24.6 us: input_part(): pl.pallas_call(functools.partial(input_kernel, count), out_shape=(jax.Sha...]
    ppermute x0 -> x32, waiting for transfers between devices: none -> 38.6 us  [the longest x18 21.3 us: col_shift(): return lax.ppermute(value, 'col', pairs)]
    ppermute x0 -> x32, starting transfers between devices: none -> 36.8 us  [the longest x18 21.2 us: col_shift(): return lax.ppermute(value, 'col', pairs)]
    dot_general x2 -> x0, matrix products: 30.8 us -> none  [the longest x1 15.6 us: local(): lax.dot_general(grad_all, weight, (((1,), (1,)), ((), ())), preferred_ele...]
    unnamed x1 -> x80, local copies, waits for them, and re-layouts: 13 us -> 10.1 us
  transfers between devices with their start and end apart: 3 -> 32, of which waited for: 3 -> 7; matrix products, arithmetic and copies ran while one was open for 15% -> 0% of each run, Pallas kernels for 0% -> 36%
where the time goes in v1:
time: 142 us
  Pallas kernels  51.3 us (36%)
  waiting for transfers between devices  38.6 us (27%)
  starting transfers between devices  36.8 us (26%)
  local copies, waits for them, and re-layouts  10.1 us (7%)
  other arithmetic  3.66 us (3%)
    pallas_call x3, Pallas kernels, input_part(): pl.pallas_call(functools.partial(input_kernel, count), out_shape=(jax.Sha...  24.6 us
    ppermute x18, waiting for transfers between devices, col_shift(): return lax.ppermute(value, 'col', pairs)  21.3 us
    ppermute x18, starting transfers between devices, col_shift(): return lax.ppermute(value, 'col', pairs)  21.2 us
    ppermute x14, waiting for transfers between devices, row_shift(): return lax.ppermute(value, 'row', pairs)  17.3 us
    pallas_call x1, Pallas kernels, weight_gradient(): pl.pallas_call(functools.partial(weight_kernel, tile), out_shape=jax.Shap...  15.9 us
    ppermute x14, starting transfers between devices, row_shift(): return lax.ppermute(value, 'row', pairs)  15.6 us
    unnamed x80, local copies, waits for them, and re-layouts  10.1 us
    pallas_call x1, Pallas kernels, transposed_tokens(): pl.pallas_call(transpose_kernel, out_shape=jax.ShapeDtypeStruct((width, r...  7.47 us
  transfers between devices with their start and end apart: 32, of which 7 were waited for; matrix products, arithmetic and copies ran while one was open for 0% of the time, Pallas kernels for 36%

profile of v1, /device:TPU:0, one launch (start us, length us, event | category | flops | bytes accessed | tf_op | source)
XLA Modules:
  0.0 141.6 jit_solution(5329946774411443263)
XLA Ops:
  3.8 2.1 %collective-permute-start.10 = (bf16[128,2048]{1,0:T(8,128)(2,1)S(1)}, bf16[128,2048]{1,0:T(8,128)(2,1)S(1)}, u32[]{:S(2)}, u32[]{:S(2)}) collective-permute-start(bf16[128,2048]{1,0:T(8,128)(2,1)S(1)} %hidden_gradient.2.refs_0_), channel_id=1, source_target_pairs={{0,16},{16,0},{32,48},{48,32},{64,80},{80,64},{96,112},{112,96},{1... | collective-permute-start | bytes 1572872 | tf_op jit(solution)/shard_map/ppermute | solution.py:30
  5.9 3.6 %collective-permute-start.24 = (bf16[64,1536]{1,0:T(8,128)(2,1)}, bf16[64,1536]{1,0:T(8,128)(2,1)S(1)}, u32[]{:S(2)}, u32[]{:S(2)}) collective-permute-start(bf16[64,1536]{1,0:T(8,128)(2,1)} %param.4), channel_id=1, source_target_pairs={{0,2},{1,3},{2,0},{3,1},{4,6},{5,7},{6,4},{7,5},{8,10},{9,11},{10,... | collective-permute-start | bytes 589832 | tf_op jit(solution)/shard_map/ppermute | solution.py:40
  9.9 3.1 %collective-permute-start.1 = (bf16[128,1024]{1,0:T(8,128)(2,1)S(1)}, bf16[128,1024]{1,0:T(8,128)(2,1)S(1)}, u32[]{:S(2)}, u32[]{:S(2)}) collective-permute-start(bf16[128,1024]{1,0:T(8,128)(2,1)S(1)} %hidden_gradient.3.refs_1_), channel_id=1, source_target_pairs={{0,96},{16,112},{32,0},{48,16},{64,32},{80,48},{96,64},{112,80},{1... | collective-permute-start | bytes 786440 | tf_op jit(solution)/shard_map/ppermute | solution.py:30
  13.0 13.4 %collective-permute-done.24 = bf16[64,1536]{1,0:T(8,128)(2,1)S(1)} collective-permute-done((bf16[64,1536]{1,0:T(8,128)(2,1)}, bf16[64,1536]{1,0:T(8,128)(2,1)S(1)}, u32[]{:S(2)}, u32[]{:S(2)}) %collective-permute-start.24) | collective-permute-done | bytes 196640 | tf_op jit(solution)/shard_map/ppermute | solution.py:40
  26.5 1.6 %collective-permute-start.2 = (bf16[128,2048]{1,0:T(8,128)(2,1)S(1)}, bf16[128,2048]{1,0:T(8,128)(2,1)S(1)}, u32[]{:S(2)}, u32[]{:S(2)}) collective-permute-start(bf16[128,2048]{1,0:T(8,128)(2,1)S(1)} %hidden_gradient.2.refs_0_), channel_id=1, source_target_pairs={{0,32},{16,48},{32,64},{48,80},{64,96},{80,112},{96,0},{112,16},{1... | collective-permute-start | bytes 1572872 | tf_op jit(solution)/shard_map/ppermute | solution.py:30
  28.0 1.7 %collective-permute-start.4 = (bf16[128,1024]{1,0:T(8,128)(2,1)S(1)}, bf16[128,1024]{1,0:T(8,128)(2,1)S(1)}, u32[]{:S(2)}, u32[]{:S(2)}) collective-permute-start(bf16[128,1024]{1,0:T(8,128)(2,1)S(1)} %collective-permute-done.1.refs_3_), channel_id=1, source_target_pairs={{0,96},{16,112},{32,0},{48,16},{64,32},{80,48},{96,64},{112,80},{1... | collective-permute-start | bytes 786440 | tf_op jit(solution)/shard_map/ppermute | solution.py:30
  29.7 1.8 %collective-permute-start.12 = (bf16[128,2048]{1,0:T(8,128)(2,1)S(1)}, bf16[128,2048]{1,0:T(8,128)(2,1)S(1)}, u32[]{:S(2)}, u32[]{:S(2)}) collective-permute-start(bf16[128,2048]{1,0:T(8,128)(2,1)S(1)} %collective-permute-done.10.refs_0_.refs_8_), channel_id=1, source_target_pairs={{0,96},{16,112},{32,0},{48,16},{64,32},{80,48},{96,64},{112,80},{1... | collective-permute-start | bytes 1572872 | tf_op jit(solution)/shard_map/ppermute | solution.py:30
  31.8 5.5 %collective-permute-done.4.refs_5_ = bf16[128,1024]{1,0:T(8,128)(2,1)S(1)} collective-permute-done((bf16[128,1024]{1,0:T(8,128)(2,1)S(1)}, bf16[128,1024]{1,0:T(8,128)(2,1)S(1)}, u32[]{:S(2)}, u32[]{:S(2)}) %collective-permute-start.4) | collective-permute-done | bytes 262176 | tf_op jit(solution)/shard_map/ppermute | solution.py:30
  37.3 2.3 %collective-permute-done.13.refs_3_.refs_11_ = bf16[128,1024]{1,0:T(8,128)(2,1)S(1)} collective-permute-done((bf16[128,1024]{1,0:T(8,128)(2,1)S(1)}, bf16[128,1024]{1,0:T(8,128)(2,1)S(1)}, u32[]{:S(2)}, u32[]{:S(2)}) %collective-permute-start.13) | collective-permute-done | bytes 262176 | tf_op jit(solution)/shard_map/ppermute | solution.py:30
  39.6 2.9 %collective-permute-start = (bf16[128,2048]{1,0:T(8,128)(2,1)S(1)}, bf16[128,2048]{1,0:T(8,128)(2,1)S(1)}, u32[]{:S(2)}, u32[]{:S(2)}) collective-permute-start(bf16[128,2048]{1,0:T(8,128)(2,1)S(1)} %hidden_gradient.2.refs_0_), channel_id=1, source_target_pairs={{0,96},{16,112},{32,0},{48,16},{64,32},{80,48},{96,64},{112,80},{1... | collective-permute-start | bytes 1572872 | tf_op jit(solution)/shard_map/ppermute | solution.py:30
  45.2 3.4 %collective-permute-done.12.refs_2_.refs_10_ = bf16[128,2048]{1,0:T(8,128)(2,1)S(1)} collective-permute-done((bf16[128,2048]{1,0:T(8,128)(2,1)S(1)}, bf16[128,2048]{1,0:T(8,128)(2,1)S(1)}, u32[]{:S(2)}, u32[]{:S(2)}) %collective-permute-start.12) | collective-permute-done | bytes 524320 | tf_op jit(solution)/shard_map/ppermute | solution.py:30
  48.5 5.2 %collective-permute-done.14.refs_4_.refs_14_ = bf16[128,2048]{1,0:T(8,128)(2,1)S(1)} collective-permute-done((bf16[128,2048]{1,0:T(8,128)(2,1)S(1)}, bf16[128,2048]{1,0:T(8,128)(2,1)S(1)}, u32[]{:S(2)}, u32[]{:S(2)}) %collective-permute-start.14) | collective-permute-done | bytes 524320 | tf_op jit(solution)/shard_map/ppermute | solution.py:30
  53.8 8.3 %input_part.4 = (f32[3,64,1536]{2,1,0:T(8,128)S(1)}, bf16[3,64,1536]{2,1,0:T(8,128)(2,1)S(1)}) custom-call(bf16[128,2048]{1,0:T(8,128)(2,1)S(1)} %collective-permute-done.10.refs_0_.refs_8_, bf16[128,1024]{1,0:T(8,128)(2,1)S(1)} %collective-permute-done.11.refs_1_.refs_9_, bf16[128,2048]{1,0:T(8,128)(2,1)S(1)} %collective-permute-done.12.refs_2_.refs_10_, ...), custom_call_target="tpu_custom_call" | custom-call | flops 3623878656 | bytes 11796480 | tf_op jit(solution)/shard_map/input_part/pallas_call | solution.py:158
  62.2 1.9 %collective-permute-start.17 = (bf16[128,2048]{1,0:T(8,128)(2,1)S(1)}, bf16[128,2048]{1,0:T(8,128)(2,1)S(1)}, u32[]{:S(2)}, u32[]{:S(2)}) collective-permute-start(bf16[128,2048]{1,0:T(8,128)(2,1)S(1)} %collective-permute-done.12.refs_2_.refs_10_), channel_id=1, source_target_pairs={{0,96},{16,112},{32,0},{48,16},{64,32},{80,48},{96,64},{112,80},{1... | collective-permute-start | bytes 1572872 | tf_op jit(solution)/shard_map/ppermute | solution.py:30
  64.2 9.2 %input_part.3 = (f32[4,64,1536]{2,1,0:T(8,128)S(1)}, bf16[4,64,1536]{2,1,0:T(8,128)(2,1)S(1)}) custom-call(bf16[128,2048]{1,0:T(8,128)(2,1)S(1)} %hidden_gradient.2.refs_0_, bf16[128,1024]{1,0:T(8,128)(2,1)S(1)} %hidden_gradient.3.refs_1_, bf16[128,2048]{1,0:T(8,128)(2,1)S(1)} %collective-permute-done.refs_2_, ...), custom_call_target="tpu_custom_call" | custom-call | flops 4831838208 | bytes 12582912 | tf_op jit(solution)/shard_map/input_part/pallas_call | solution.py:158
  73.7 3.0 %collective-permute-start.26 = (bf16[2,64,1536]{2,1,0:T(8,128)(2,1)S(1)}, bf16[2,64,1536]{2,1,0:T(8,128)(2,1)S(1)}, u32[]{:S(2)}, u32[]{:S(2)}) collective-permute-start(bf16[2,64,1536]{2,1,0:T(8,128)(2,1)S(1)} %pad_maximum_fusion.refs_0_), channel_id=1, source_target_pairs={{0,8},{1,9},{2,10},{3,11},{4,12},{5,13},{6,14},{7,15},{8,0},{9,1},... | collective-permute-start | bytes 1179656 | tf_op jit(solution)/shard_map/ppermute | solution.py:40
  76.7 2.6 %collective-permute-start.27 = (bf16[2,64,1536]{2,1,0:T(8,128)(2,1)S(1)}, bf16[2,64,1536]{2,1,0:T(8,128)(2,1)S(1)}, u32[]{:S(2)}, u32[]{:S(2)}) collective-permute-start(bf16[2,64,1536]{2,1,0:T(8,128)(2,1)S(1)} %pad_maximum_fusion.refs_0_), channel_id=1, source_target_pairs={{0,12},{1,13},{2,14},{3,15},{4,0},{5,1},{6,2},{7,3},{8,4},{9,5},{1... | collective-permute-start | bytes 1179656 | tf_op jit(solution)/shard_map/ppermute | solution.py:40
  79.3 7.2 %input_part.5 = (f32[1,64,1536]{2,1,0:T(8,128)S(1)}, bf16[1,64,1536]{2,1,0:T(8,128)(2,1)S(1)}) custom-call(bf16[128,2048]{1,0:T(8,128)(2,1)S(1)} %collective-permute-done.17.refs_0_.refs_12_, bf16[128,1024]{1,0:T(8,128)(2,1)S(1)} %collective-permute-done.18.refs_1_.refs_13_, bf16[1536,3072]{1,0:T(8,128)(2,1)} %refs_2_.1), custom_call_target="tpu_custom_call" | custom-call | flops 1207959552 | bytes 10223616 | tf_op jit(solution)/shard_map/input_part/pallas_call | solution.py:158
  87.2 7.9 %collective-permute-done.27.refs_3_ = bf16[2,64,1536]{2,1,0:T(8,128)(2,1)S(1)} collective-permute-done((bf16[2,64,1536]{2,1,0:T(8,128)(2,1)S(1)}, bf16[2,64,1536]{2,1,0:T(8,128)(2,1)S(1)}, u32[]{:S(2)}, u32[]{:S(2)}) %collective-permute-start.27) | collective-permute-done | bytes 393248 | tf_op jit(solution)/shard_map/ppermute | solution.py:40
  99.7 2.7 %collective-permute-start.21 = (bf16[64,1536]{1,0:T(8,128)(2,1)}, bf16[64,1536]{1,0:T(8,128)(2,1)}, u32[]{:S(2)}, u32[]{:S(2)}) collective-permute-start(bf16[64,1536]{1,0:T(8,128)(2,1)} %get-tuple-element.28), channel_id=1, source_target_pairs={{0,8},{1,9},{2,10},{3,11},{4,12},{5,13},{6,14},{7,15},{8,0},{9,1},... | collective-permute-start | bytes 589832 | tf_op jit(solution)/shard_map/ppermute | solution.py:40
  108.3 1.9 %collective-permute-start.9 = (bf16[64,1536]{1,0:T(8,128)(2,1)}, bf16[64,1536]{1,0:T(8,128)(2,1)}, u32[]{:S(2)}, u32[]{:S(2)}) collective-permute-start(bf16[64,1536]{1,0:T(8,128)(2,1)} %get-tuple-element.21), channel_id=1, source_target_pairs={{0,12},{1,13},{2,14},{3,15},{4,0},{5,1},{6,2},{7,3},{8,4},{9,5},{1... | collective-permute-start | bytes 589832 | tf_op jit(solution)/shard_map/ppermute | solution.py:40
  114.3 7.5 %transposed_tokens.1.refs_16_ = bf16[1536,1024]{1,0:T(8,128)(2,1)} custom-call(bf16[2,64,1536]{2,1,0:T(8,128)(2,1)S(1)} %pad_maximum_fusion.refs_0_, bf16[2,64,1536]{2,1,0:T(8,128)(2,1)S(1)} %collective-permute-done.25.refs_1_, bf16[2,64,1536]{2,1,0:T(8,128)(2,1)S(1)} %collective-permute-done.26.refs_2_, ...), custom_call_target="tpu_custom_call" | custom-call | bytes 12582912 | tf_op jit(solution)/shard_map/transposed_tokens/pallas_call | solution.py:98
  123.5 15.9 %weight_gradient.1 = bf16[1536,3072]{1,0:T(8,128)(2,1)} custom-call(bf16[128,2048]{1,0:T(8,128)(2,1)S(1)} %hidden_gradient.2.refs_0_, bf16[128,1024]{1,0:T(8,128)(2,1)S(1)} %copy-done.11, bf16[128,2048]{1,0:T(8,128)(2,1)S(1)} %copy-done.22, bf16[128,1024]{1,0:T(8,128)(2,1)S(1)} %copy-done.26, bf16[128,2048]{1,0:T(8,128)(2,1)S(1)} %copy-done.24, ...), custom_call_target="tpu_custom_call" | custom-call | flops 9663676416 | bytes 9437184 | tf_op jit(solution)/shard_map/weight_gradient/pallas_call | solution.py:251
  139.4 2.2 %add_convert_fusion = bf16[64,1536]{1,0:T(8,128)(2,1)} fusion(bf16[64,1536]{1,0:T(8,128)(2,1)S(1)} %collective-permute-done.23, pred[]{:T(512)S(6)} %eq.6, bf16[64,1536]{1,0:T(8,128)(2,1)} %collective-permute-done.9, bf16[64,1536]{1,0:T(8,128)(2,1)} %collective-permute-done.8, f32[64,1536]{1,0:T(8,128)S(1)} %get-tuple-element.18, ...), kind=kLoop, calls=%fused_computation.1 | loop fusion | flops 1572864 | bytes 2359297 | tf_op jit(solution)/shard_map/convert_element_type | solution.py:310
  (132 shorter events, 23.7 us)
Async XLA Ops:
  3.8 25.9 %collective-permute-start.10 = (bf16[128,2048]{1,0:T(8,128)(2,1)S(1)}, bf16[128,2048]{1,0:T(8,128)(2,1)S(1)}, u32[]{:S(2)}, u32[]{:S(2)}) collective-permute-start(bf16[128,2048]{1,0:T(8,128)(2,1)S(1)} %hidden_gradient.2.refs_0_), channel_id=1, source_target_pairs={{0,16},{16,0},{32,48},{48,32},{64,80},{80,64},{96,112},{112,96},{1... | collective-permute-start | bytes 1572872 | tf_op jit(solution)/shard_map/ppermute | solution.py:30
  5.9 20.6 %collective-permute-start.24 = (bf16[64,1536]{1,0:T(8,128)(2,1)}, bf16[64,1536]{1,0:T(8,128)(2,1)S(1)}, u32[]{:S(2)}, u32[]{:S(2)}) collective-permute-start(bf16[64,1536]{1,0:T(8,128)(2,1)} %param.4), channel_id=1, source_target_pairs={{0,2},{1,3},{2,0},{3,1},{4,6},{5,7},{6,4},{7,5},{8,10},{9,11},{10,... | collective-permute-start | bytes 589832 | tf_op jit(solution)/shard_map/ppermute | solution.py:40
  9.9 18.1 %collective-permute-start.1 = (bf16[128,1024]{1,0:T(8,128)(2,1)S(1)}, bf16[128,1024]{1,0:T(8,128)(2,1)S(1)}, u32[]{:S(2)}, u32[]{:S(2)}) collective-permute-start(bf16[128,1024]{1,0:T(8,128)(2,1)S(1)} %hidden_gradient.3.refs_1_), channel_id=1, source_target_pairs={{0,96},{16,112},{32,0},{48,16},{64,32},{80,48},{96,64},{112,80},{1... | collective-permute-start | bytes 786440 | tf_op jit(solution)/shard_map/ppermute | solution.py:30
  13.0 18.5 %collective-permute-start.5 = (bf16[128,1024]{1,0:T(8,128)(2,1)S(1)}, bf16[128,1024]{1,0:T(8,128)(2,1)S(1)}, u32[]{:S(2)}, u32[]{:S(2)}) collective-permute-start(bf16[128,1024]{1,0:T(8,128)(2,1)S(1)} %hidden_gradient.3.refs_1_), channel_id=1, source_target_pairs={{0,32},{16,48},{32,64},{48,80},{64,96},{80,112},{96,0},{112,16},{1... | collective-permute-start | bytes 786440 | tf_op jit(solution)/shard_map/ppermute | solution.py:30
  13.0 18.7 %collective-permute-start.11 = (bf16[128,1024]{1,0:T(8,128)(2,1)S(1)}, bf16[128,1024]{1,0:T(8,128)(2,1)S(1)}, u32[]{:S(2)}, u32[]{:S(2)}) collective-permute-start(bf16[128,1024]{1,0:T(8,128)(2,1)S(1)} %hidden_gradient.3.refs_1_), channel_id=1, source_target_pairs={{0,16},{16,0},{32,48},{48,32},{64,80},{80,64},{96,112},{112,96},{1... | collective-permute-start | bytes 786440 | tf_op jit(solution)/shard_map/ppermute | solution.py:30
  26.5 16.1 %collective-permute-start.2 = (bf16[128,2048]{1,0:T(8,128)(2,1)S(1)}, bf16[128,2048]{1,0:T(8,128)(2,1)S(1)}, u32[]{:S(2)}, u32[]{:S(2)}) collective-permute-start(bf16[128,2048]{1,0:T(8,128)(2,1)S(1)} %hidden_gradient.2.refs_0_), channel_id=1, source_target_pairs={{0,32},{16,48},{32,64},{48,80},{64,96},{80,112},{96,0},{112,16},{1... | collective-permute-start | bytes 1572872 | tf_op jit(solution)/shard_map/ppermute | solution.py:30
  29.7 18.8 %collective-permute-start.12 = (bf16[128,2048]{1,0:T(8,128)(2,1)S(1)}, bf16[128,2048]{1,0:T(8,128)(2,1)S(1)}, u32[]{:S(2)}, u32[]{:S(2)}) collective-permute-start(bf16[128,2048]{1,0:T(8,128)(2,1)S(1)} %collective-permute-done.10.refs_0_.refs_8_), channel_id=1, source_target_pairs={{0,96},{16,112},{32,0},{48,16},{64,32},{80,48},{96,64},{112,80},{1... | collective-permute-start | bytes 1572872 | tf_op jit(solution)/shard_map/ppermute | solution.py:30
  31.5 22.2 %collective-permute-start.14 = (bf16[128,2048]{1,0:T(8,128)(2,1)S(1)}, bf16[128,2048]{1,0:T(8,128)(2,1)S(1)}, u32[]{:S(2)}, u32[]{:S(2)}) collective-permute-start(bf16[128,2048]{1,0:T(8,128)(2,1)S(1)} %collective-permute-done.10.refs_0_.refs_8_), channel_id=1, source_target_pairs={{0,32},{16,48},{32,64},{48,80},{64,96},{80,112},{96,0},{112,16},{1... | collective-permute-start | bytes 1572872 | tf_op jit(solution)/shard_map/ppermute | solution.py:30
  39.6 22.6 %collective-permute-start = (bf16[128,2048]{1,0:T(8,128)(2,1)S(1)}, bf16[128,2048]{1,0:T(8,128)(2,1)S(1)}, u32[]{:S(2)}, u32[]{:S(2)}) collective-permute-start(bf16[128,2048]{1,0:T(8,128)(2,1)S(1)} %hidden_gradient.2.refs_0_), channel_id=1, source_target_pairs={{0,96},{16,112},{32,0},{48,16},{64,32},{80,48},{96,64},{112,80},{1... | collective-permute-start | bytes 1572872 | tf_op jit(solution)/shard_map/ppermute | solution.py:30
  42.5 21.6 %collective-permute-start.3 = (bf16[128,2048]{1,0:T(8,128)(2,1)S(1)}, bf16[128,2048]{1,0:T(8,128)(2,1)S(1)}, u32[]{:S(2)}, u32[]{:S(2)}) collective-permute-start(bf16[128,2048]{1,0:T(8,128)(2,1)S(1)} %collective-permute-done.2.refs_6_), channel_id=1, source_target_pairs={{0,32},{16,48},{32,64},{48,80},{64,96},{80,112},{96,0},{112,16},{1... | collective-permute-start | bytes 1572872 | tf_op jit(solution)/shard_map/ppermute | solution.py:30
  43.7 42.9 %collective-permute-start.25 = (bf16[2,64,1536]{2,1,0:T(8,128)(2,1)S(1)}, bf16[2,64,1536]{2,1,0:T(8,128)(2,1)S(1)}, u32[]{:S(2)}, u32[]{:S(2)}) collective-permute-start(bf16[2,64,1536]{2,1,0:T(8,128)(2,1)S(1)} %pad_maximum_fusion.refs_0_), channel_id=1, source_target_pairs={{0,4},{1,5},{2,6},{3,7},{4,8},{5,9},{6,10},{7,11},{8,12},{9,13},{1... | collective-permute-start | bytes 1179656 | tf_op jit(solution)/shard_map/ppermute | solution.py:40
  48.5 25.1 %collective-permute-start.18 = (bf16[128,1024]{1,0:T(8,128)(2,1)S(1)}, bf16[128,1024]{1,0:T(8,128)(2,1)S(1)}, u32[]{:S(2)}, u32[]{:S(2)}) collective-permute-start(bf16[128,1024]{1,0:T(8,128)(2,1)S(1)} %collective-permute-done.4.refs_5_), channel_id=1, source_target_pairs={{0,16},{16,0},{32,48},{48,32},{64,80},{80,64},{96,112},{112,96},{1... | collective-permute-start | bytes 786440 | tf_op jit(solution)/shard_map/ppermute | solution.py:30
  62.1 32.9 %collective-permute-start.16 = (bf16[3,64,1536]{2,1,0:T(8,128)(2,1)S(1)}, bf16[3,64,1536]{2,1,0:T(8,128)(2,1)S(1)}, u32[]{:S(2)}, u32[]{:S(2)}) collective-permute-start(bf16[3,64,1536]{2,1,0:T(8,128)(2,1)S(1)} %get-tuple-element.23), channel_id=1, source_target_pairs={{0,1},{1,0},{2,3},{3,2},{4,5},{5,4},{6,7},{7,6},{8,9},{9,8},{10,11... | collective-permute-start | bytes 1769480 | tf_op jit(solution)/shard_map/ppermute | solution.py:40
  62.2 14.5 %collective-permute-start.17 = (bf16[128,2048]{1,0:T(8,128)(2,1)S(1)}, bf16[128,2048]{1,0:T(8,128)(2,1)S(1)}, u32[]{:S(2)}, u32[]{:S(2)}) collective-permute-start(bf16[128,2048]{1,0:T(8,128)(2,1)S(1)} %collective-permute-done.12.refs_2_.refs_10_), channel_id=1, source_target_pairs={{0,96},{16,112},{32,0},{48,16},{64,32},{80,48},{96,64},{112,80},{1... | collective-permute-start | bytes 1572872 | tf_op jit(solution)/shard_map/ppermute | solution.py:30
  73.4 23.3 %collective-permute-start.6 = (bf16[4,64,1536]{2,1,0:T(8,128)(2,1)S(1)}, bf16[4,64,1536]{2,1,0:T(8,128)(2,1)S(1)}, u32[]{:S(2)}, u32[]{:S(2)}) collective-permute-start(bf16[4,64,1536]{2,1,0:T(8,128)(2,1)S(1)} %get-tuple-element.17), channel_id=1, source_target_pairs={{0,1},{1,0},{2,3},{3,2},{4,5},{5,4},{6,7},{7,6},{8,9},{9,8},{10,11... | collective-permute-start | bytes 2359304 | tf_op jit(solution)/shard_map/ppermute | solution.py:40
  73.7 13.0 %collective-permute-start.26 = (bf16[2,64,1536]{2,1,0:T(8,128)(2,1)S(1)}, bf16[2,64,1536]{2,1,0:T(8,128)(2,1)S(1)}, u32[]{:S(2)}, u32[]{:S(2)}) collective-permute-start(bf16[2,64,1536]{2,1,0:T(8,128)(2,1)S(1)} %pad_maximum_fusion.refs_0_), channel_id=1, source_target_pairs={{0,8},{1,9},{2,10},{3,11},{4,12},{5,13},{6,14},{7,15},{8,0},{9,1},... | collective-permute-start | bytes 1179656 | tf_op jit(solution)/shard_map/ppermute | solution.py:40
  76.7 18.3 %collective-permute-start.27 = (bf16[2,64,1536]{2,1,0:T(8,128)(2,1)S(1)}, bf16[2,64,1536]{2,1,0:T(8,128)(2,1)S(1)}, u32[]{:S(2)}, u32[]{:S(2)}) collective-permute-start(bf16[2,64,1536]{2,1,0:T(8,128)(2,1)S(1)} %pad_maximum_fusion.refs_0_), channel_id=1, source_target_pairs={{0,12},{1,13},{2,14},{3,15},{4,0},{5,1},{6,2},{7,3},{8,4},{9,5},{1... | collective-permute-start | bytes 1179656 | tf_op jit(solution)/shard_map/ppermute | solution.py:40
  86.7 12.3 %collective-permute-start.28 = (bf16[2,64,1536]{2,1,0:T(8,128)(2,1)S(1)}, bf16[2,64,1536]{2,1,0:T(8,128)(2,1)S(1)}, u32[]{:S(2)}, u32[]{:S(2)}) collective-permute-start(bf16[2,64,1536]{2,1,0:T(8,128)(2,1)S(1)} %pad_maximum_fusion.refs_0_), channel_id=1, source_target_pairs={{0,1},{1,0},{2,3},{3,2},{4,5},{5,4},{6,7},{7,6},{8,9},{9,8},{10,11... | collective-permute-start | bytes 1179656 | tf_op jit(solution)/shard_map/ppermute | solution.py:40
  99.7 22.0 %collective-permute-start.21 = (bf16[64,1536]{1,0:T(8,128)(2,1)}, bf16[64,1536]{1,0:T(8,128)(2,1)}, u32[]{:S(2)}, u32[]{:S(2)}) collective-permute-start(bf16[64,1536]{1,0:T(8,128)(2,1)} %get-tuple-element.28), channel_id=1, source_target_pairs={{0,8},{1,9},{2,10},{3,11},{4,12},{5,13},{6,14},{7,15},{8,0},{9,1},... | collective-permute-start | bytes 589832 | tf_op jit(solution)/shard_map/ppermute | solution.py:40
  103.2 18.5 %collective-permute-start.22 = (bf16[64,1536]{1,0:T(8,128)(2,1)}, bf16[64,1536]{1,0:T(8,128)(2,1)}, u32[]{:S(2)}, u32[]{:S(2)}) collective-permute-start(bf16[64,1536]{1,0:T(8,128)(2,1)} %get-tuple-element.29), channel_id=1, source_target_pairs={{0,12},{1,13},{2,14},{3,15},{4,0},{5,1},{6,2},{7,3},{8,4},{9,5},{1... | collective-permute-start | bytes 589832 | tf_op jit(solution)/shard_map/ppermute | solution.py:40
  104.6 17.2 %collective-permute-start.7 = (bf16[64,1536]{1,0:T(8,128)(2,1)}, bf16[64,1536]{1,0:T(8,128)(2,1)}, u32[]{:S(2)}, u32[]{:S(2)}) collective-permute-start(bf16[64,1536]{1,0:T(8,128)(2,1)} %get-tuple-element.19), channel_id=1, source_target_pairs={{0,4},{1,5},{2,6},{3,7},{4,8},{5,9},{6,10},{7,11},{8,12},{9,13},{1... | collective-permute-start | bytes 589832 | tf_op jit(solution)/shard_map/ppermute | solution.py:40
  106.8 15.0 %collective-permute-start.8 = (bf16[64,1536]{1,0:T(8,128)(2,1)}, bf16[64,1536]{1,0:T(8,128)(2,1)}, u32[]{:S(2)}, u32[]{:S(2)}) collective-permute-start(bf16[64,1536]{1,0:T(8,128)(2,1)} %get-tuple-element.20), channel_id=1, source_target_pairs={{0,8},{1,9},{2,10},{3,11},{4,12},{5,13},{6,14},{7,15},{8,0},{9,1},... | collective-permute-start | bytes 589832 | tf_op jit(solution)/shard_map/ppermute | solution.py:40
  108.3 13.5 %collective-permute-start.9 = (bf16[64,1536]{1,0:T(8,128)(2,1)}, bf16[64,1536]{1,0:T(8,128)(2,1)}, u32[]{:S(2)}, u32[]{:S(2)}) collective-permute-start(bf16[64,1536]{1,0:T(8,128)(2,1)} %get-tuple-element.21), channel_id=1, source_target_pairs={{0,12},{1,13},{2,14},{3,15},{4,0},{5,1},{6,2},{7,3},{8,4},{9,5},{1... | collective-permute-start | bytes 589832 | tf_op jit(solution)/shard_map/ppermute | solution.py:40
  123.3 16.1 %collective-permute-start.23 = (bf16[64,1536]{1,0:T(8,128)(2,1)S(1)}, bf16[64,1536]{1,0:T(8,128)(2,1)S(1)}, u32[]{:S(2)}, u32[]{:S(2)}) collective-permute-start(bf16[64,1536]{1,0:T(8,128)(2,1)S(1)} %select_convert_fusion), channel_id=1, source_target_pairs={{0,2},{1,3},{2,0},{3,1},{4,6},{5,7},{6,4},{7,5},{8,10},{9,11},{10,... | collective-permute-start | bytes 589832 | tf_op jit(solution)/shard_map/ppermute | solution.py:40
  (48 other events, 577.8 us)

commit v2 on v1

v2 whole, which is shorter than its diff:
```python
import functools
import math

import jax
import jax.numpy as jnp
from jax import lax
from jax.experimental import pallas as pl
from jax.experimental.pallas import tpu as pltpu
from jax.sharding import PartitionSpec as P

BF, F32 = jnp.bfloat16, jnp.float32
LIMIT = 32 * 1024 * 1024
WHOLE = 60 * 1024 * 1024


def params(limit=LIMIT):
    return pltpu.CompilerParams(vmem_limit_bytes=limit)


def cost(flops, bytes_accessed):
    return pl.CostEstimate(
        flops=flops, bytes_accessed=bytes_accessed, transcendentals=0
    )


def place():
    row, col = lax.axis_index("row"), lax.axis_index("col")
    return row // 2, row % 2, col // 4, (col // 2) % 2, col % 2


def row_shift(value, dy, dz=0):
    pairs = [(y * 2 + z, ((y + dy) % 4) * 2 + (z + dz) % 2) for y in range(4) for z in range(2)]
    return lax.ppermute(value, "row", pairs)


def col_shift(value, dx, dh=0, dk=0):
    pairs = [
        (x * 4 + h * 2 + k, ((x + dx) % 4) * 4 + ((h + dh) % 2) * 2 + (k + dk) % 2)
        for x in range(4)
        for h in range(2)
        for k in range(2)
    ]
    return lax.ppermute(value, "col", pairs)


def after(value, *others):
    return lax.optimization_barrier((value, *others))[0]


def slope_kernel(pre_ref, up_ref, out_ref):
    value = pre_ref[...].astype(F32)
    scale = math.sqrt(2.0 / math.pi)
    square = value * value
    tangent = jnp.tanh(scale * (value + 0.044715 * value * square))
    slope = 0.5 * (1.0 + tangent) + 0.5 * value * (1.0 - tangent * tangent) * scale * (
        1.0 + 3.0 * 0.044715 * square
    )
    out_ref[...] = (up_ref[...].astype(F32) * slope).astype(BF)


def hidden_gradient(pre_act, upstream, step=1024):
    rows, width = pre_act.shape
    spec = pl.BlockSpec((rows, step), lambda j: (0, j))
    return pl.pallas_call(
        slope_kernel,
        out_shape=jax.ShapeDtypeStruct((rows, width), BF),
        grid=(width // step,),
        in_specs=[spec, spec],
        out_specs=spec,
        compiler_params=params(),
        cost_estimate=cost(30 * rows * width, 6 * rows * width),
        name="hidden_gradient",
    )(pre_act, upstream)


def transpose_kernel(*refs):
    pieces, (out_ref, whole, sem) = refs[:4], refs[4:]
    _, _, x, h, _ = place()
    copies = []
    for shift, piece in enumerate(pieces):
        owner = (x + 4 - shift) % 4
        for dh in range(2):
            offset = (owner * 2 + (h + dh) % 2) * 64
            copies.append(
                pltpu.make_async_copy(
                    piece.at[dh],
                    whole.at[pl.ds(pl.multiple_of(offset, 64), 64), :],
                    sem.at[shift, dh],
                )
            )
    for copy in copies:
        copy.start()
    for copy in copies:
        copy.wait()
    for start in range(0, whole.shape[1], 256):
        out_ref[start : start + 256, :] = whole[:, start : start + 256].T


def transposed_tokens(pieces):
    width = pieces[0].shape[2]
    rows = 8 * 64
    return pl.pallas_call(
        transpose_kernel,
        out_shape=jax.ShapeDtypeStruct((width, rows), BF),
        grid=(1,),
        in_specs=[pl.BlockSpec(memory_space=pl.ANY)] * 4,
        out_specs=pl.BlockSpec((width, rows), lambda j: (0, 0)),
        scratch_shapes=[pltpu.VMEM((rows, width), BF), pltpu.SemaphoreType.DMA((4, 2))],
        compiler_params=params(),
        cost_estimate=cost(0, 8 * rows * width),
        name="transposed_tokens",
    )(*pieces)


def hold_kernel(weight_ref, out_ref, sem):
    step = weight_ref.shape[0] // 4
    copies = [
        pltpu.make_async_copy(
            weight_ref.at[pl.ds(i * step, step), :], out_ref.at[pl.ds(i * step, step), :], sem.at[i]
        )
        for i in range(4)
    ]
    for copy in copies:
        copy.start()
    for copy in copies:
        copy.wait()


def held_weight(weight):
    return pl.pallas_call(
        hold_kernel,
        out_shape=pltpu.VMEM(weight.shape, weight.dtype),
        in_specs=[pl.BlockSpec(memory_space=pl.ANY)],
        out_specs=pl.BlockSpec(memory_space=pltpu.VMEM),
        scratch_shapes=[pltpu.SemaphoreType.DMA((4,))],
        compiler_params=params(),
        cost_estimate=cost(0, 2 * weight.size * 2),
        name="held_weight",
    )(weight)


def input_kernel(layout, *refs):
    count = len(layout)
    pieces, weight_ref, (own_ref, send_ref, held, sem) = refs[:count], refs[count], refs[count + 1 :]
    core = lax.axis_index("col") % 2

    @pl.when(pl.program_id(0) == 0)
    def _():
        copies, at = [], 0
        for number, rows in enumerate(layout):
            copies.append(
                pltpu.make_async_copy(pieces[number], held.at[pl.ds(at, rows), :], sem.at[number])
            )
            at += rows
        for copy in copies:
            copy.start()
        for copy in copies:
            copy.wait()

    step = own_ref.shape[2]
    part = weight_ref[pl.ds(pl.multiple_of(pl.program_id(0) * step, step), step), :]
    total = lax.dot_general(
        held[...], part, (((1,), (1,)), ((), ())), preferred_element_type=F32
    )
    total = total.reshape(own_ref.shape[0], 2, 64, total.shape[1])

    @pl.when(core == 0)
    def _():
        own_ref[...] = total[:, 0]
        send_ref[...] = total[:, 1].astype(BF)

    @pl.when(core == 1)
    def _():
        own_ref[...] = total[:, 1]
        send_ref[...] = total[:, 0].astype(BF)


def input_part(blocks, weight, step=768):
    count = len(blocks)
    features, hidden = weight.shape
    pieces = [piece for block in blocks for piece in block]
    layout = tuple(piece.shape[0] for piece in pieces)
    spec = pl.BlockSpec((count, 64, step), lambda j: (0, 0, j))
    return pl.pallas_call(
        functools.partial(input_kernel, layout),
        out_shape=(
            jax.ShapeDtypeStruct((count, 64, features), F32),
            jax.ShapeDtypeStruct((count, 64, features), BF),
        ),
        grid=(features // step,),
        in_specs=[pl.BlockSpec(memory_space=pl.ANY)] * len(pieces)
        + [pl.BlockSpec(memory_space=pltpu.VMEM)],
        out_specs=(spec, spec),
        scratch_shapes=[
            pltpu.VMEM((count * 128, hidden), BF),
            pltpu.SemaphoreType.DMA((len(pieces),)),
        ],
        compiler_params=params(),
        cost_estimate=cost(
            2 * count * 128 * features * hidden, 2 * features * hidden + 2 * count * 128 * hidden
        ),
        name="input_part",
    )(*pieces, weight)


def deal_kernel(places, *refs):
    count = len(places)
    ins, outs, both = refs[: 2 * count], refs[2 * count : 2 * count + 4], refs[-1]
    y, _, x, _, _ = place()
    for number, group in enumerate(places):
        own, received = ins[2 * number], ins[2 * number + 1]
        for at, dy in group:
            both[dy] = own[at] + received[at].astype(F32)
    for dx in range(4):
        outs[dx][...] = both[(x + dx + 4 - y) % 4].astype(outs[dx].dtype)


def dealt(places, arrays, limit, step=768):
    rows, features = arrays[0].shape[1:]
    spec = pl.BlockSpec((rows, step), lambda j: (0, j))
    return pl.pallas_call(
        functools.partial(deal_kernel, places),
        out_shape=[jax.ShapeDtypeStruct((rows, features), F32)]
        + [jax.ShapeDtypeStruct((rows, features), BF)] * 3,
        grid=(features // step,),
        in_specs=[
            pl.BlockSpec((array.shape[0], rows, step), lambda j: (0, 0, j)) for array in arrays
        ],
        out_specs=[spec] * 4,
        scratch_shapes=[pltpu.VMEM((4, rows, step), F32)],
        compiler_params=params(limit),
        cost_estimate=cost(0, 40 * rows * features),
        name="dealt",
    )(*arrays)


def weight_kernel(tile, first, count, halves, *refs):
    arrays = len(set(number for half in halves for number, _ in half))
    pieces, (mine_ref, other_ref) = refs[:arrays], refs[arrays : arrays + 2]
    out_ref, held, tokens, sem, token_sem = refs[-5:]
    y, z, _, _, core = place()
    j = pl.program_id(0)

    def copies(group):
        made = []
        start, width = (0, tile) if group == 0 else (tile, (count - 1) * tile)
        for block, half in enumerate(halves):
            owner = ((y + block % 4) % 4) * 2 + (z + block // 4) % 2
            for side, (number, row) in enumerate(half):
                made.append(
                    pltpu.make_async_copy(
                        pieces[number].at[pl.ds(row, 64), pl.ds(first * tile + start, width)],
                        held.at[
                            pl.ds(pl.multiple_of(side * 512 + owner * 64, 64), 64),
                            pl.ds(start, width),
                        ],
                        sem.at[block * 2 + side, group],
                    )
                )
        return made

    def token_copies():
        return [
            pltpu.make_async_copy(
                ref, tokens.at[:, pl.ds(pl.multiple_of(side * 512, 512), 512)], token_sem.at[number]
            )
            for number, (ref, side) in enumerate(((mine_ref, core), (other_ref, 1 - core)))
        ]

    @pl.when(j == 0)
    def _():
        made = token_copies() + copies(0)
        for copy in made + copies(1):
            copy.start()
        for copy in made:
            copy.wait()

    @pl.when(j == 1)
    def _():
        for copy in copies(1):
            copy.wait()

    out_ref[...] = jnp.dot(
        tokens[...],
        held[:, pl.ds(pl.multiple_of(j * tile, tile), tile)],
        preferred_element_type=F32,
    ).astype(BF)


def weight_gradient(mine, other, blocks, hidden, first, count, before=None, tile=512):
    features, rows = mine.shape[0], 2 * mine.shape[1]
    pieces = [piece for block in blocks for piece in block]
    halves, number = [], 0
    for block in blocks:
        if len(block) == 1:
            halves.append(((number, 0), (number, 64)))
        else:
            halves.append(((number, 0), (number + 1, 0)))
        number += len(block)
    operands = [*pieces, mine, other]
    aliases = {}
    if before is not None:
        aliases = {len(operands): 0}
        operands.append(before)
    return pl.pallas_call(
        functools.partial(weight_kernel, tile, first, count, tuple(halves)),
        out_shape=jax.ShapeDtypeStruct((features, hidden), BF),
        grid=(count,),
        in_specs=[pl.BlockSpec(memory_space=pl.ANY)] * len(operands),
        out_specs=pl.BlockSpec((features, tile), lambda j: (0, first + j)),
        scratch_shapes=[
            pltpu.VMEM((rows, count * tile), BF),
            pltpu.VMEM((features, rows), BF),
            pltpu.SemaphoreType.DMA((16, 2)),
            pltpu.SemaphoreType.DMA((2,)),
        ],
        input_output_aliases=aliases,
        compiler_params=params(WHOLE),
        cost_estimate=cost(3 * rows * features * count * tile, 2 * features * count * tile),
        name="weight_gradient",
    )(*operands)


def local(tokens, weight, pre_act, upstream):
    y, z, x, h, core = place()
    hidden = pre_act.shape[1]

    own = hidden_gradient(pre_act, upstream)
    up, down, across = row_shift(own, 1), row_shift(own, -1), row_shift(own, 0, 1)

    pair = jnp.stack([tokens, col_shift(tokens, 0, 1)])
    mine = [pair] + [col_shift(pair, dx) for dx in (1, 2, 3)]
    tokens_mine = transposed_tokens(mine)
    tokens_other = col_shift(tokens_mine, 0, 0, 1)

    far_y = row_shift(up, 1)
    up_z = row_shift(after(up, across), 0, 1)
    down_z = row_shift(after(across, down), -1)
    far_z = (row_shift(up_z[:64], 1), row_shift(down_z[64:], -1))

    near = [(own,), (down,), (far_y,), (up,)]
    far = [(across,), (down_z,), far_z, (up_z,)]

    weight = held_weight(weight)
    own1, send1 = input_part([near[0], near[1], near[3], far[0]], weight)
    got1 = col_shift(send1, 0, 0, 1)
    own2, send2 = input_part([near[2], far[1], far[3]], weight)
    got2 = col_shift(send2, 0, 0, 1)
    s0, s1, s2, s3 = dealt((((0, 0), (1, 1), (2, 3)), ((0, 2),)), [own1, got1, own2, got2], LIMIT)
    r1, r2, r3 = col_shift(s1, 1), col_shift(s2, 2), col_shift(s3, 3)

    own3, send3 = input_part([(after(far_z[0], s1), far_z[1])], weight)
    got3 = after(col_shift(send3, 0, 0, 1), r1, r2, r3)
    t0, t1, t2, t3 = dealt(
        (((3, 0),), ((1, 1), (2, 3)), ((0, 2),)), [own1, got1, own2, got2, own3, got3], WHOLE
    )
    v1, v2, v3 = col_shift(t1, 1), col_shift(t2, 2), col_shift(t3, 3)

    tokens_other = after(tokens_other, t1)
    weight_grad = weight_gradient(tokens_mine, tokens_other, near + far, hidden, 0, 4)
    t0, weight_grad = lax.optimization_barrier((t0, weight_grad))

    sum1 = s0 + r1.astype(F32) + r2.astype(F32) + r3.astype(F32)
    sum2 = t0 + v1.astype(F32) + v2.astype(F32) + v3.astype(F32)
    owner = h == z
    last = jnp.where(owner, sum2, sum1).astype(BF)
    last, weight_grad = lax.optimization_barrier((last, weight_grad))
    last = col_shift(last, 0, 1)
    weight_grad = weight_gradient(
        tokens_mine, tokens_other, near + far, hidden, 4, 2, weight_grad
    )
    input_grad = (jnp.where(owner, sum1, sum2) + last.astype(F32)).astype(BF)
    return (input_grad, weight_grad)


def solution(mesh):
    in_specs = (P("col", "row"), P("row", "col"), P("row", "col"), P("row", "col"))
    out_specs = (P("col", "row"), P("row", "col"))
    return jax.shard_map(local, mesh=mesh, in_specs=in_specs, out_specs=out_specs, check_vma=False)
```

time: 142 us -> 109 us (0.77)
  waiting for transfers between devices: 38.6 us -> 22.6 us
  Pallas kernels: 51.3 us -> 43.2 us
  starting transfers between devices: 36.8 us -> 32.4 us
  local copies, waits for them, and re-layouts: 10.1 us -> 7.51 us
  other arithmetic: 3.66 us -> 2.03 us
    ppermute x18 -> x15, waiting for transfers between devices: 21.3 us -> 6.75 us  [col_shift(): return lax.ppermute(value, 'col', pairs)]
    ppermute x14 -> x8, starting transfers between devices: 15.6 us -> 10.6 us  [row_shift(): return lax.ppermute(value, 'row', pairs)]
    pallas_call x1, Pallas kernels: 7.47 us -> 2.61 us  [transposed_tokens(): pl.pallas_call(transpose_kernel, out_shape=jax.ShapeDtypeStruct((width, r...]
    pallas_call x6 -> x8, Pallas kernels: 42.5 us -> 39.4 us  [the longest x2 20 us: weight_gradient(): pl.pallas_call(functools.partial(weight_kernel, tile, first, count, tuple...]
    unnamed x80 -> x44, local copies, waits for them, and re-layouts: 10.1 us -> 7.46 us
    ppermute x14 -> x8, waiting for transfers between devices: 17.3 us -> 15.9 us  [row_shift(): return lax.ppermute(value, 'row', pairs)]
    ppermute x18 -> x15, starting transfers between devices: 21.2 us -> 21.8 us  [col_shift(): return lax.ppermute(value, 'col', pairs)]
  transfers between devices with their start and end apart: 32 -> 23, of which waited for: 7 -> 6; matrix products, arithmetic and copies ran while one was open for 0% -> 1% of each run, Pallas kernels for 36% -> 39%
where the time goes in v2:
time: 109 us
  Pallas kernels  43.2 us (40%)
  starting transfers between devices  32.4 us (30%)
  waiting for transfers between devices  22.6 us (21%)
  local copies, waits for them, and re-layouts  7.51 us (7%)
  other arithmetic  2.03 us (2%)
    ppermute x15, starting transfers between devices, col_shift(): return lax.ppermute(value, 'col', pairs)  21.8 us
    pallas_call x2, Pallas kernels, weight_gradient(): pl.pallas_call(functools.partial(weight_kernel, tile, first, count, tuple...  20 us
    ppermute x8, waiting for transfers between devices, row_shift(): return lax.ppermute(value, 'row', pairs)  15.9 us
    pallas_call x3, Pallas kernels, input_part(): pl.pallas_call(functools.partial(input_kernel, layout), out_shape=(jax.Sh...  14.2 us
    ppermute x8, starting transfers between devices, row_shift(): return lax.ppermute(value, 'row', pairs)  10.6 us
    unnamed x44, local copies, waits for them, and re-layouts  7.46 us
    ppermute x15, waiting for transfers between devices, col_shift(): return lax.ppermute(value, 'col', pairs)  6.75 us
    pallas_call x2, Pallas kernels, dealt(): pl.pallas_call(functools.partial(deal_kernel, places), out_shape=[jax.Sha...  4.54 us
  transfers between devices with their start and end apart: 23, of which 6 were waited for; matrix products, arithmetic and copies ran while one was open for 1% of the time, Pallas kernels for 39%

profile of v2, /device:TPU:0, one launch (start us, length us, event | category | flops | bytes accessed | tf_op | source)
XLA Modules:
  0.0 108.9 jit_solution(3565511533926912752)
XLA Ops:
  4.2 3.2 %collective-permute-start = (bf16[128,3072]{1,0:T(8,128)(2,1)S(1)}, bf16[128,3072]{1,0:T(8,128)(2,1)S(1)}, u32[]{:S(2)}, u32[]{:S(2)}) collective-permute-start(bf16[128,3072]{1,0:T(8,128)(2,1)S(1)} %hidden_gradient.1.refs_0_), channel_id=1, source_target_pairs={{0,96},{16,112},{32,0},{48,16},{64,32},{80,48},{96,64},{112,80},{1... | collective-permute-start | bytes 2359304 | tf_op jit(solution)/shard_map/ppermute | solution.py:33
  7.3 3.9 %collective-permute-start.14 = (bf16[64,1536]{1,0:T(8,128)(2,1)}, bf16[64,1536]{1,0:T(8,128)(2,1)S(1)}, u32[]{:S(2)}, u32[]{:S(2)}) collective-permute-start(bf16[64,1536]{1,0:T(8,128)(2,1)} %param.4), channel_id=1, source_target_pairs={{0,2},{1,3},{2,0},{3,1},{4,6},{5,7},{6,4},{7,5},{8,10},{9,11},{10,... | collective-permute-start | bytes 589832 | tf_op jit(solution)/shard_map/ppermute | solution.py:43
  12.2 5.0 %collective-permute-done.14 = bf16[64,1536]{1,0:T(8,128)(2,1)S(1)} collective-permute-done((bf16[64,1536]{1,0:T(8,128)(2,1)}, bf16[64,1536]{1,0:T(8,128)(2,1)S(1)}, u32[]{:S(2)}, u32[]{:S(2)}) %collective-permute-start.14) | collective-permute-done | bytes 196640 | tf_op jit(solution)/shard_map/ppermute | solution.py:43
  18.2 1.6 %collective-permute-start.15 = (bf16[2,64,1536]{2,1,0:T(8,128)(2,1)S(1)}, bf16[2,64,1536]{2,1,0:T(8,128)(2,1)S(1)}, u32[]{:S(2)}, u32[]{:S(2)}) collective-permute-start(bf16[2,64,1536]{2,1,0:T(8,128)(2,1)S(1)} %pad_maximum_fusion.refs_0_), channel_id=1, source_target_pairs={{0,4},{1,5},{2,6},{3,7},{4,8},{5,9},{6,10},{7,11},{8,12},{9,13},{1... | collective-permute-start | bytes 1179656 | tf_op jit(solution)/shard_map/ppermute | solution.py:43
  19.7 2.7 %collective-permute-start.16 = (bf16[2,64,1536]{2,1,0:T(8,128)(2,1)S(1)}, bf16[2,64,1536]{2,1,0:T(8,128)(2,1)S(1)}, u32[]{:S(2)}, u32[]{:S(2)}) collective-permute-start(bf16[2,64,1536]{2,1,0:T(8,128)(2,1)S(1)} %pad_maximum_fusion.refs_0_), channel_id=1, source_target_pairs={{0,8},{1,9},{2,10},{3,11},{4,12},{5,13},{6,14},{7,15},{8,0},{9,1},... | collective-permute-start | bytes 1179656 | tf_op jit(solution)/shard_map/ppermute | solution.py:43
  22.4 1.7 %collective-permute-done.refs_1_ = bf16[128,3072]{1,0:T(8,128)(2,1)S(1)} collective-permute-done((bf16[128,3072]{1,0:T(8,128)(2,1)S(1)}, bf16[128,3072]{1,0:T(8,128)(2,1)S(1)}, u32[]{:S(2)}, u32[]{:S(2)}) %collective-permute-start) | collective-permute-done | bytes 786464 | tf_op jit(solution)/shard_map/ppermute | solution.py:33
  24.1 2.8 %collective-permute-start.17 = (bf16[2,64,1536]{2,1,0:T(8,128)(2,1)S(1)}, bf16[2,64,1536]{2,1,0:T(8,128)(2,1)S(1)}, u32[]{:S(2)}, u32[]{:S(2)}) collective-permute-start(bf16[2,64,1536]{2,1,0:T(8,128)(2,1)S(1)} %pad_maximum_fusion.refs_0_), channel_id=1, source_target_pairs={{0,12},{1,13},{2,14},{3,15},{4,0},{5,1},{6,2},{7,3},{8,4},{9,5},{1... | collective-permute-start | bytes 1179656 | tf_op jit(solution)/shard_map/ppermute | solution.py:43
  26.9 6.7 %collective-permute-done.2.refs_3_.refs_4_ = bf16[128,3072]{1,0:T(8,128)(2,1)S(1)} collective-permute-done((bf16[128,3072]{1,0:T(8,128)(2,1)S(1)}, bf16[128,3072]{1,0:T(8,128)(2,1)S(1)}, u32[]{:S(2)}, u32[]{:S(2)}) %collective-permute-start.2) | collective-permute-done | bytes 786464 | tf_op jit(solution)/shard_map/ppermute | solution.py:33
  36.7 3.7 %copy-done = bf16[1536,3072]{1,0:T(8,128)(2,1)S(1)} copy-done((bf16[1536,3072]{1,0:T(8,128)(2,1)S(1)}, bf16[1536,3072]{1,0:T(8,128)(2,1)}, u32[]{:S(2)}) %copy-start) | copy-done | bytes 9437208
  41.1 2.6 %transposed_tokens.1.refs_9_ = bf16[1536,512]{1,0:T(8,128)(2,1)S(1)} custom-call(bf16[2,64,1536]{2,1,0:T(8,128)(2,1)S(1)} %pad_maximum_fusion.refs_0_, bf16[2,64,1536]{2,1,0:T(8,128)(2,1)S(1)} %collective-permute-done.15.refs_1_, bf16[2,64,1536]{2,1,0:T(8,128)(2,1)S(1)} %collective-permute-done.16.refs_2_, ...), custom_call_target="tpu_custom_call" | custom-call | bytes 6291456 | tf_op jit(solution)/shard_map/transposed_tokens/pallas_call | solution.py:102
  43.8 5.9 %input_part.3 = (f32[4,64,1536]{2,1,0:T(8,128)S(1)}, bf16[4,64,1536]{2,1,0:T(8,128)(2,1)S(1)}) custom-call(bf16[128,3072]{1,0:T(8,128)(2,1)S(1)} %hidden_gradient.1.refs_0_, bf16[128,3072]{1,0:T(8,128)(2,1)S(1)} %collective-permute-done.refs_1_, bf16[128,3072]{1,0:T(8,128)(2,1)S(1)} %collective-permute-done.1.refs_2_.refs_3_, ...), custom_call_target="tpu_custom_call" | custom-call | flops 4831838208 | bytes 12582912 | tf_op jit(solution)/shard_map/input_part/pallas_call | solution.py:184
  50.3 3.1 %collective-permute-done.4.refs_0_.refs_2_ = bf16[128,3072]{1,0:T(8,128)(2,1)S(1)} collective-permute-done((bf16[128,3072]{1,0:T(8,128)(2,1)S(1)}, bf16[128,3072]{1,0:T(8,128)(2,1)S(1)}, u32[]{:S(2)}, u32[]{:S(2)}) %collective-permute-start.4) | collective-permute-done | bytes 786464 | tf_op jit(solution)/shard_map/ppermute | solution.py:33
  53.4 4.5 %input_part.4 = (f32[3,64,1536]{2,1,0:T(8,128)S(1)}, bf16[3,64,1536]{2,1,0:T(8,128)(2,1)S(1)}) custom-call(bf16[128,3072]{1,0:T(8,128)(2,1)S(1)} %collective-permute-done.4.refs_0_.refs_2_, bf16[128,3072]{1,0:T(8,128)(2,1)S(1)} %collective-permute-done.5.refs_1_.refs_5_, bf16[128,3072]{1,0:T(8,128)(2,1)S(1)} %collective-permute-done.6.refs_2_.refs_8_, ...), custom_call_target="tpu_custom_call" | custom-call | flops 3623878656 | bytes 11796480 | tf_op jit(solution)/shard_map/input_part/pallas_call | solution.py:184
  58.3 3.2 %collective-permute-start.12 = (bf16[64,3072]{1,0:T(8,128)(2,1)S(1)}, bf16[64,3072]{1,0:T(8,128)(2,1)S(1)}, u32[]{:S(2)}, u32[]{:S(2)}) collective-permute-start(bf16[64,3072]{1,0:T(8,128)(2,1)S(1)} %slice.9), channel_id=1, source_target_pairs={{0,96},{16,112},{32,0},{48,16},{64,32},{80,48},{96,64},{112,80},{1... | collective-permute-start | bytes 1179656 | tf_op jit(solution)/shard_map/ppermute | solution.py:33
  62.9 2.8 %collective-permute-start.10 = (bf16[64,1536]{1,0:T(8,128)(2,1)}, bf16[64,1536]{1,0:T(8,128)(2,1)S(1)}, u32[]{:S(2)}, u32[]{:S(2)}) collective-permute-start(bf16[64,1536]{1,0:T(8,128)(2,1)} %get-tuple-element.34), channel_id=1, source_target_pairs={{0,12},{1,13},{2,14},{3,15},{4,0},{5,1},{6,2},{7,3},{8,4},{9,5},{1... | collective-permute-start | bytes 589832 | tf_op jit(solution)/shard_map/ppermute | solution.py:43
  66.5 4.4 %collective-permute-done.11.refs_0_.refs_6_ = bf16[64,3072]{1,0:T(8,128)(2,1)S(1)} collective-permute-done((bf16[64,3072]{1,0:T(8,128)(2,1)S(1)}, bf16[64,3072]{1,0:T(8,128)(2,1)S(1)}, u32[]{:S(2)}, u32[]{:S(2)}) %collective-permute-start.11) | collective-permute-done | bytes 393248 | tf_op jit(solution)/shard_map/ppermute | solution.py:33
  70.9 1.5 %collective-permute-start.8 = (bf16[64,1536]{1,0:T(8,128)(2,1)}, bf16[64,1536]{1,0:T(8,128)(2,1)S(1)}, u32[]{:S(2)}, u32[]{:S(2)}) collective-permute-start(bf16[64,1536]{1,0:T(8,128)(2,1)} %get-tuple-element.32), channel_id=1, source_target_pairs={{0,4},{1,5},{2,6},{3,7},{4,8},{5,9},{6,10},{7,11},{8,12},{9,13},{1... | collective-permute-start | bytes 589832 | tf_op jit(solution)/shard_map/ppermute | solution.py:43
  72.4 3.8 %input_part.5 = (f32[1,64,1536]{2,1,0:T(8,128)S(1)}, bf16[1,64,1536]{2,1,0:T(8,128)(2,1)S(1)}) custom-call(bf16[64,3072]{1,0:T(8,128)(2,1)S(1)} %collective-permute-done.11.refs_0_.refs_6_, bf16[64,3072]{1,0:T(8,128)(2,1)S(1)} %collective-permute-done.12.refs_1_.refs_7_, bf16[1536,3072]{1,0:T(8,128)(2,1)S(1)} %held_weight.1.refs_4_.refs_3_.refs_2_), custom_call_target="tpu_custom_call" | custom-call | flops 1207959552 | bytes 10223616 | tf_op jit(solution)/shard_map/input_part/pallas_call | solution.py:184
  77.1 1.8 %collective-permute-done.8 = bf16[64,1536]{1,0:T(8,128)(2,1)S(1)} collective-permute-done((bf16[64,1536]{1,0:T(8,128)(2,1)}, bf16[64,1536]{1,0:T(8,128)(2,1)S(1)}, u32[]{:S(2)}, u32[]{:S(2)}) %collective-permute-start.8) | collective-permute-done | bytes 196640 | tf_op jit(solution)/shard_map/ppermute | solution.py:43
  79.5 3.2 %dealt.3 = (f32[64,1536]{1,0:T(8,128)}, bf16[64,1536]{1,0:T(8,128)(2,1)}, bf16[64,1536]{1,0:T(8,128)(2,1)}, bf16[64,1536]{1,0:T(8,128)(2,1)}) custom-call(f32[4,64,1536]{2,1,0:T(8,128)} %copy-done.2, bf16[4,64,1536]{2,1,0:T(8,128)(2,1)} %copy-done.5, f32[3,64,1536]{2,1,0:T(8,128)} %copy-done.3, bf16[3,64,1536]{2,1,0:T(8,128)(2,1)} %copy-done.6, ...), custom_call_target="tpu_custom_call" | custom-call | bytes 3932160 | tf_op jit(solution)/shard_map/dealt/pallas_call | solution.py:221
  82.7 1.6 %collective-permute-start.21 = (bf16[64,1536]{1,0:T(8,128)(2,1)}, bf16[64,1536]{1,0:T(8,128)(2,1)S(1)}, u32[]{:S(2)}, u32[]{:S(2)}) collective-permute-start(bf16[64,1536]{1,0:T(8,128)(2,1)} %get-tuple-element.44), channel_id=1, source_target_pairs={{0,12},{1,13},{2,14},{3,15},{4,0},{5,1},{6,2},{7,3},{8,4},{9,5},{1... | collective-permute-start | bytes 589832 | tf_op jit(solution)/shard_map/ppermute | solution.py:43
  84.3 1.6 %collective-permute-start.20 = (bf16[64,1536]{1,0:T(8,128)(2,1)}, bf16[64,1536]{1,0:T(8,128)(2,1)S(1)}, u32[]{:S(2)}, u32[]{:S(2)}) collective-permute-start(bf16[64,1536]{1,0:T(8,128)(2,1)} %get-tuple-element.43), channel_id=1, source_target_pairs={{0,8},{1,9},{2,10},{3,11},{4,12},{5,13},{6,14},{7,15},{8,0},{9,1},... | collective-permute-start | bytes 589832 | tf_op jit(solution)/shard_map/ppermute | solution.py:43
  86.5 12.2 %weight_gradient.2.refs_11_ = bf16[1536,3072]{1,0:T(8,128)(2,1)} custom-call(bf16[128,3072]{1,0:T(8,128)(2,1)} %copy-done.4, bf16[128,3072]{1,0:T(8,128)(2,1)} %copy-done.13, bf16[128,3072]{1,0:T(8,128)(2,1)} %copy-done.16, bf16[128,3072]{1,0:T(8,128)(2,1)} %copy-done.15, bf16[128,3072]{1,0:T(8,128)(2,1)} %copy-done.14, bf16[128,3072]{1,0:T(8,128)(2,1)} %copy-done.7, ...), custom_call_target="tpu_custom_call" | custom-call | flops 9663676416 | bytes 6291456 | tf_op jit(solution)/shard_map/weight_gradient/pallas_call | solution.py:305
  100.2 7.8 %weight_gradient.3 = bf16[1536,3072]{1,0:T(8,128)(2,1)} custom-call(bf16[128,3072]{1,0:T(8,128)(2,1)} %copy-done.4, bf16[128,3072]{1,0:T(8,128)(2,1)} %copy-done.13, bf16[128,3072]{1,0:T(8,128)(2,1)} %copy-done.16, bf16[128,3072]{1,0:T(8,128)(2,1)} %copy-done.15, bf16[128,3072]{1,0:T(8,128)(2,1)} %copy-done.14, ...), custom_call_target="tpu_custom_call", output_to_operand_aliasing={{}: (11, {})} | custom-call | flops 4831838208 | bytes 3145728 | tf_op jit(solution)/shard_map/weight_gradient/pallas_call | solution.py:305
  (81 shorter events, 16.8 us)
Async XLA Ops:
  4.2 39.6 %copy-start.4 = (bf16[128,3072]{1,0:T(8,128)(2,1)}, bf16[128,3072]{1,0:T(8,128)(2,1)S(1)}, u32[]{:S(2)}) copy-start(bf16[128,3072]{1,0:T(8,128)(2,1)S(1)} %hidden_gradient.1.refs_0_) | copy-start | bytes 2359300
  4.2 20.0 %collective-permute-start = (bf16[128,3072]{1,0:T(8,128)(2,1)S(1)}, bf16[128,3072]{1,0:T(8,128)(2,1)S(1)}, u32[]{:S(2)}, u32[]{:S(2)}) collective-permute-start(bf16[128,3072]{1,0:T(8,128)(2,1)S(1)} %hidden_gradient.1.refs_0_), channel_id=1, source_target_pairs={{0,96},{16,112},{32,0},{48,16},{64,32},{80,48},{96,64},{112,80},{1... | collective-permute-start | bytes 2359304 | tf_op jit(solution)/shard_map/ppermute | solution.py:33
  7.3 9.9 %collective-permute-start.14 = (bf16[64,1536]{1,0:T(8,128)(2,1)}, bf16[64,1536]{1,0:T(8,128)(2,1)S(1)}, u32[]{:S(2)}, u32[]{:S(2)}) collective-permute-start(bf16[64,1536]{1,0:T(8,128)(2,1)} %param.4), channel_id=1, source_target_pairs={{0,2},{1,3},{2,0},{3,1},{4,6},{5,7},{6,4},{7,5},{8,10},{9,11},{10,... | collective-permute-start | bytes 589832 | tf_op jit(solution)/shard_map/ppermute | solution.py:43
  11.2 22.4 %collective-permute-start.2 = (bf16[128,3072]{1,0:T(8,128)(2,1)S(1)}, bf16[128,3072]{1,0:T(8,128)(2,1)S(1)}, u32[]{:S(2)}, u32[]{:S(2)}) collective-permute-start(bf16[128,3072]{1,0:T(8,128)(2,1)S(1)} %hidden_gradient.1.refs_0_), channel_id=1, source_target_pairs={{0,16},{16,0},{32,48},{48,32},{64,80},{80,64},{96,112},{112,96},{1... | collective-permute-start | bytes 2359304 | tf_op jit(solution)/shard_map/ppermute | solution.py:33
  12.2 22.1 %collective-permute-start.1 = (bf16[128,3072]{1,0:T(8,128)(2,1)S(1)}, bf16[128,3072]{1,0:T(8,128)(2,1)S(1)}, u32[]{:S(2)}, u32[]{:S(2)}) collective-permute-start(bf16[128,3072]{1,0:T(8,128)(2,1)S(1)} %hidden_gradient.1.refs_0_), channel_id=1, source_target_pairs={{0,32},{16,48},{32,64},{48,80},{64,96},{80,112},{96,0},{112,16},{1... | collective-permute-start | bytes 2359304 | tf_op jit(solution)/shard_map/ppermute | solution.py:33
  18.2 17.5 %collective-permute-start.15 = (bf16[2,64,1536]{2,1,0:T(8,128)(2,1)S(1)}, bf16[2,64,1536]{2,1,0:T(8,128)(2,1)S(1)}, u32[]{:S(2)}, u32[]{:S(2)}) collective-permute-start(bf16[2,64,1536]{2,1,0:T(8,128)(2,1)S(1)} %pad_maximum_fusion.refs_0_), channel_id=1, source_target_pairs={{0,4},{1,5},{2,6},{3,7},{4,8},{5,9},{6,10},{7,11},{8,12},{9,13},{1... | collective-permute-start | bytes 1179656 | tf_op jit(solution)/shard_map/ppermute | solution.py:43
  19.7 21.3 %collective-permute-start.16 = (bf16[2,64,1536]{2,1,0:T(8,128)(2,1)S(1)}, bf16[2,64,1536]{2,1,0:T(8,128)(2,1)S(1)}, u32[]{:S(2)}, u32[]{:S(2)}) collective-permute-start(bf16[2,64,1536]{2,1,0:T(8,128)(2,1)S(1)} %pad_maximum_fusion.refs_0_), channel_id=1, source_target_pairs={{0,8},{1,9},{2,10},{3,11},{4,12},{5,13},{6,14},{7,15},{8,0},{9,1},... | collective-permute-start | bytes 1179656 | tf_op jit(solution)/shard_map/ppermute | solution.py:43
  24.1 16.9 %collective-permute-start.17 = (bf16[2,64,1536]{2,1,0:T(8,128)(2,1)S(1)}, bf16[2,64,1536]{2,1,0:T(8,128)(2,1)S(1)}, u32[]{:S(2)}, u32[]{:S(2)}) collective-permute-start(bf16[2,64,1536]{2,1,0:T(8,128)(2,1)S(1)} %pad_maximum_fusion.refs_0_), channel_id=1, source_target_pairs={{0,12},{1,13},{2,14},{3,15},{4,0},{5,1},{6,2},{7,3},{8,4},{9,5},{1... | collective-permute-start | bytes 1179656 | tf_op jit(solution)/shard_map/ppermute | solution.py:43
  33.6 19.8 %collective-permute-start.5 = (bf16[128,3072]{1,0:T(8,128)(2,1)S(1)}, bf16[128,3072]{1,0:T(8,128)(2,1)S(1)}, u32[]{:S(2)}, u32[]{:S(2)}) collective-permute-start(bf16[128,3072]{1,0:T(8,128)(2,1)S(1)} %collective-permute-done.2.refs_3_.refs_4_), channel_id=1, source_target_pairs={{0,96},{16,112},{32,0},{48,16},{64,32},{80,48},{96,64},{112,80},{1... | collective-permute-start | bytes 2359304 | tf_op jit(solution)/shard_map/ppermute | solution.py:33
  34.4 19.0 %collective-permute-start.4 = (bf16[128,3072]{1,0:T(8,128)(2,1)S(1)}, bf16[128,3072]{1,0:T(8,128)(2,1)S(1)}, u32[]{:S(2)}, u32[]{:S(2)}) collective-permute-start(bf16[128,3072]{1,0:T(8,128)(2,1)S(1)} %collective-permute-done.1.refs_2_.refs_3_), channel_id=1, source_target_pairs={{0,32},{16,48},{32,64},{48,80},{64,96},{80,112},{96,0},{112,16},{1... | collective-permute-start | bytes 2359304 | tf_op jit(solution)/shard_map/ppermute | solution.py:33
  35.7 17.7 %collective-permute-start.6 = (bf16[128,3072]{1,0:T(8,128)(2,1)S(1)}, bf16[128,3072]{1,0:T(8,128)(2,1)S(1)}, u32[]{:S(2)}, u32[]{:S(2)}) collective-permute-start(bf16[128,3072]{1,0:T(8,128)(2,1)S(1)} %collective-permute-done.1.refs_2_.refs_3_), channel_id=1, source_target_pairs={{0,16},{16,0},{32,48},{48,32},{64,80},{80,64},{96,112},{112,96},{1... | collective-permute-start | bytes 2359304 | tf_op jit(solution)/shard_map/ppermute | solution.py:33
  43.7 42.8 %collective-permute-start.18 = (bf16[1536,512]{1,0:T(8,128)(2,1)S(1)}, bf16[1536,512]{1,0:T(8,128)(2,1)}, u32[]{:S(2)}, u32[]{:S(2)}) collective-permute-start(bf16[1536,512]{1,0:T(8,128)(2,1)S(1)} %transposed_tokens.1.refs_9_), channel_id=1, source_target_pairs={{0,1},{1,0},{2,3},{3,2},{4,5},{5,4},{6,7},{7,6},{8,9},{9,8},{10,11... | collective-permute-start | bytes 4718600 | tf_op jit(solution)/shard_map/ppermute | solution.py:43
  49.7 11.8 %collective-permute-start.3 = (bf16[4,64,1536]{2,1,0:T(8,128)(2,1)S(1)}, bf16[4,64,1536]{2,1,0:T(8,128)(2,1)S(1)}, u32[]{:S(2)}, u32[]{:S(2)}) collective-permute-start(bf16[4,64,1536]{2,1,0:T(8,128)(2,1)S(1)} %get-tuple-element.26), channel_id=1, source_target_pairs={{0,1},{1,0},{2,3},{3,2},{4,5},{5,4},{6,7},{7,6},{8,9},{9,8},{10,11... | collective-permute-start | bytes 2359304 | tf_op jit(solution)/shard_map/ppermute | solution.py:43
  58.0 3.5 %collective-permute-start.7 = (bf16[3,64,1536]{2,1,0:T(8,128)(2,1)S(1)}, bf16[3,64,1536]{2,1,0:T(8,128)(2,1)S(1)}, u32[]{:S(2)}, u32[]{:S(2)}) collective-permute-start(bf16[3,64,1536]{2,1,0:T(8,128)(2,1)S(1)} %get-tuple-element.30), channel_id=1, source_target_pairs={{0,1},{1,0},{2,3},{3,2},{4,5},{5,4},{6,7},{7,6},{8,9},{9,8},{10,11... | collective-permute-start | bytes 1769480 | tf_op jit(solution)/shard_map/ppermute | solution.py:43
  58.1 12.8 %collective-permute-start.11 = (bf16[64,3072]{1,0:T(8,128)(2,1)S(1)}, bf16[64,3072]{1,0:T(8,128)(2,1)S(1)}, u32[]{:S(2)}, u32[]{:S(2)}) collective-permute-start(bf16[64,3072]{1,0:T(8,128)(2,1)S(1)} %slice.8), channel_id=1, source_target_pairs={{0,32},{16,48},{32,64},{48,80},{64,96},{80,112},{96,0},{112,16},{1... | collective-permute-start | bytes 1179656 | tf_op jit(solution)/shard_map/ppermute | solution.py:33
  58.3 14.1 %collective-permute-start.12 = (bf16[64,3072]{1,0:T(8,128)(2,1)S(1)}, bf16[64,3072]{1,0:T(8,128)(2,1)S(1)}, u32[]{:S(2)}, u32[]{:S(2)}) collective-permute-start(bf16[64,3072]{1,0:T(8,128)(2,1)S(1)} %slice.9), channel_id=1, source_target_pairs={{0,96},{16,112},{32,0},{48,16},{64,32},{80,48},{96,64},{112,80},{1... | collective-permute-start | bytes 1179656 | tf_op jit(solution)/shard_map/ppermute | solution.py:33
  62.9 14.1 %collective-permute-start.10 = (bf16[64,1536]{1,0:T(8,128)(2,1)}, bf16[64,1536]{1,0:T(8,128)(2,1)S(1)}, u32[]{:S(2)}, u32[]{:S(2)}) collective-permute-start(bf16[64,1536]{1,0:T(8,128)(2,1)} %get-tuple-element.34), channel_id=1, source_target_pairs={{0,12},{1,13},{2,14},{3,15},{4,0},{5,1},{6,2},{7,3},{8,4},{9,5},{1... | collective-permute-start | bytes 589832 | tf_op jit(solution)/shard_map/ppermute | solution.py:43
  65.7 11.3 %collective-permute-start.9 = (bf16[64,1536]{1,0:T(8,128)(2,1)}, bf16[64,1536]{1,0:T(8,128)(2,1)S(1)}, u32[]{:S(2)}, u32[]{:S(2)}) collective-permute-start(bf16[64,1536]{1,0:T(8,128)(2,1)} %get-tuple-element.33), channel_id=1, source_target_pairs={{0,8},{1,9},{2,10},{3,11},{4,12},{5,13},{6,14},{7,15},{8,0},{9,1},... | collective-permute-start | bytes 589832 | tf_op jit(solution)/shard_map/ppermute | solution.py:43
  70.9 7.9 %collective-permute-start.8 = (bf16[64,1536]{1,0:T(8,128)(2,1)}, bf16[64,1536]{1,0:T(8,128)(2,1)S(1)}, u32[]{:S(2)}, u32[]{:S(2)}) collective-permute-start(bf16[64,1536]{1,0:T(8,128)(2,1)} %get-tuple-element.32), channel_id=1, source_target_pairs={{0,4},{1,5},{2,6},{3,7},{4,8},{5,9},{6,10},{7,11},{8,12},{9,13},{1... | collective-permute-start | bytes 589832 | tf_op jit(solution)/shard_map/ppermute | solution.py:43
  77.0 1.9 %collective-permute-start.13 = (bf16[1,64,1536]{2,1,0:T(8,128)(2,1)S(1)}, bf16[1,64,1536]{2,1,0:T(8,128)(2,1)S(1)}, u32[]{:S(2)}, u32[]{:S(2)}) collective-permute-start(bf16[1,64,1536]{2,1,0:T(8,128)(2,1)S(1)} %get-tuple-element.37), channel_id=1, source_target_pairs={{0,1},{1,0},{2,3},{3,2},{4,5},{5,4},{6,7},{7,6},{8,9},{9,8},{10,11... | collective-permute-start | bytes 589832 | tf_op jit(solution)/shard_map/ppermute | solution.py:43
  82.7 16.0 %collective-permute-start.21 = (bf16[64,1536]{1,0:T(8,128)(2,1)}, bf16[64,1536]{1,0:T(8,128)(2,1)S(1)}, u32[]{:S(2)}, u32[]{:S(2)}) collective-permute-start(bf16[64,1536]{1,0:T(8,128)(2,1)} %get-tuple-element.44), channel_id=1, source_target_pairs={{0,12},{1,13},{2,14},{3,15},{4,0},{5,1},{6,2},{7,3},{8,4},{9,5},{1... | collective-permute-start | bytes 589832 | tf_op jit(solution)/shard_map/ppermute | solution.py:43
  84.3 14.4 %collective-permute-start.20 = (bf16[64,1536]{1,0:T(8,128)(2,1)}, bf16[64,1536]{1,0:T(8,128)(2,1)S(1)}, u32[]{:S(2)}, u32[]{:S(2)}) collective-permute-start(bf16[64,1536]{1,0:T(8,128)(2,1)} %get-tuple-element.43), channel_id=1, source_target_pairs={{0,8},{1,9},{2,10},{3,11},{4,12},{5,13},{6,14},{7,15},{8,0},{9,1},... | collective-permute-start | bytes 589832 | tf_op jit(solution)/shard_map/ppermute | solution.py:43
  85.9 12.8 %collective-permute-start.19 = (bf16[64,1536]{1,0:T(8,128)(2,1)}, bf16[64,1536]{1,0:T(8,128)(2,1)S(1)}, u32[]{:S(2)}, u32[]{:S(2)}) collective-permute-start(bf16[64,1536]{1,0:T(8,128)(2,1)} %get-tuple-element.40), channel_id=1, source_target_pairs={{0,4},{1,5},{2,6},{3,7},{4,8},{5,9},{6,10},{7,11},{8,12},{9,13},{1... | collective-permute-start | bytes 589832 | tf_op jit(solution)/shard_map/ppermute | solution.py:43
  98.9 9.1 %collective-permute-start.22 = (bf16[64,1536]{1,0:T(8,128)(2,1)S(1)}, bf16[64,1536]{1,0:T(8,128)(2,1)S(1)}, u32[]{:S(2)}, u32[]{:S(2)}) collective-permute-start(bf16[64,1536]{1,0:T(8,128)(2,1)S(1)} %select_convert_fusion), channel_id=1, source_target_pairs={{0,2},{1,3},{2,0},{3,1},{4,6},{5,7},{6,4},{7,5},{8,10},{9,11},{10,... | collective-permute-start | bytes 589832 | tf_op jit(solution)/shard_map/ppermute | solution.py:43
  (21 other events, 211.7 us)

commit v3 on v2

--- a/solution.py
+++ b/solution.py
@@ -10,7 +10,7 @@
 
 BF, F32 = jnp.bfloat16, jnp.float32
 LIMIT = 32 * 1024 * 1024
-WHOLE = 60 * 1024 * 1024
+WHOLE = 40 * 1024 * 1024
 
 
 def params(limit=LIMIT):
@@ -112,6 +112,34 @@
     )(*pieces)
 
 
+def side_kernel(mine_ref, other_ref, out_ref, sem):
+    core = lax.axis_index("col") % 2
+    copies = [
+        pltpu.make_async_copy(
+            ref, out_ref.at[:, pl.ds(pl.multiple_of(side * 512, 512), 512)], sem.at[number]
+        )
+        for number, (ref, side) in enumerate(((mine_ref, core), (other_ref, 1 - core)))
+    ]
+    for copy in copies:
+        copy.start()
+    for copy in copies:
+        copy.wait()
+
+
+def held_tokens(mine, other):
+    features, rows = mine.shape
+    return pl.pallas_call(
+        side_kernel,
+        out_shape=pltpu.VMEM((features, 2 * rows), BF),
+        in_specs=[pl.BlockSpec(memory_space=pl.ANY)] * 2,
+        out_specs=pl.BlockSpec(memory_space=pltpu.VMEM),
+        scratch_shapes=[pltpu.SemaphoreType.DMA((2,))],
+        compiler_params=params(),
+        cost_estimate=cost(0, 8 * features * rows),
+        name="held_tokens",
+    )(mine, other)
+
+
 def hold_kernel(weight_ref, out_ref, sem):
     step = weight_ref.shape[0] // 4
     copies = [
@@ -203,29 +231,29 @@
     )(*pieces, weight)
 
 
-def deal_kernel(places, *refs):
-    count = len(places)
+def deal_kernel(order, *refs):
+    count = len(order)
     ins, outs, both = refs[: 2 * count], refs[2 * count : 2 * count + 4], refs[-1]
     y, _, x, _, _ = place()
-    for number, group in enumerate(places):
-        own, received = ins[2 * number], ins[2 * number + 1]
-        for at, dy in group:
-            both[dy] = own[at] + received[at].astype(F32)
+    for number, dy in enumerate(order):
+        both[dy] = ins[2 * number][0] + ins[2 * number + 1][0].astype(F32)
     for dx in range(4):
         outs[dx][...] = both[(x + dx + 4 - y) % 4].astype(outs[dx].dtype)
 
 
-def dealt(places, arrays, limit, step=768):
-    rows, features = arrays[0].shape[1:]
+def dealt(blocks, limit, step=768):
+    rows, features = blocks[0][0].shape[1:]
     spec = pl.BlockSpec((rows, step), lambda j: (0, j))
-    return pl.pallas_call(
-        functools.partial(deal_kernel, places),
+    arrays, specs = [], []
+    for own, received, at in blocks:
+        arrays += [own, received]
+        specs += [pl.BlockSpec((1, rows, step), lambda j, at=at: (at, 0, j))] * 2
+    return pl.pallas_call(
+        functools.partial(deal_kernel, range(len(blocks))),
         out_shape=[jax.ShapeDtypeStruct((rows, features), F32)]
         + [jax.ShapeDtypeStruct((rows, features), BF)] * 3,
         grid=(features // step,),
-        in_specs=[
-            pl.BlockSpec((array.shape[0], rows, step), lambda j: (0, 0, j)) for array in arrays
-        ],
+        in_specs=specs,
         out_specs=[spec] * 4,
         scratch_shapes=[pltpu.VMEM((4, rows, step), F32)],
         compiler_params=params(limit),
@@ -234,61 +262,27 @@
     )(*arrays)
 
 
-def weight_kernel(tile, first, count, halves, *refs):
-    arrays = len(set(number for half in halves for number, _ in half))
-    pieces, (mine_ref, other_ref) = refs[:arrays], refs[arrays : arrays + 2]
-    out_ref, held, tokens, sem, token_sem = refs[-5:]
-    y, z, _, _, core = place()
-    j = pl.program_id(0)
-
-    def copies(group):
-        made = []
-        start, width = (0, tile) if group == 0 else (tile, (count - 1) * tile)
-        for block, half in enumerate(halves):
-            owner = ((y + block % 4) % 4) * 2 + (z + block // 4) % 2
-            for side, (number, row) in enumerate(half):
-                made.append(
-                    pltpu.make_async_copy(
-                        pieces[number].at[pl.ds(row, 64), pl.ds(first * tile + start, width)],
-                        held.at[
-                            pl.ds(pl.multiple_of(side * 512 + owner * 64, 64), 64),
-                            pl.ds(start, width),
-                        ],
-                        sem.at[block * 2 + side, group],
-                    )
+def rows_kernel(halves, *refs):
+    pieces, (out_ref, sem) = refs[:-2], refs[-2:]
+    y, z, _, _, _ = place()
+    copies = []
+    for block, half in enumerate(halves):
+        owner = ((y + block % 4) % 4) * 2 + (z + block // 4) % 2
+        for side, (number, row) in enumerate(half):
+            copies.append(
+                pltpu.make_async_copy(
+                    pieces[number].at[pl.ds(row, 64), :],
+                    out_ref.at[pl.ds(pl.multiple_of(side * 512 + owner * 64, 64), 64), :],
+                    sem.at[block * 2 + side],
                 )
-        return made
-
-    def token_copies():
-        return [
-            pltpu.make_async_copy(
-                ref, tokens.at[:, pl.ds(pl.multiple_of(side * 512, 512), 512)], token_sem.at[number]
             )
-            for number, (ref, side) in enumerate(((mine_ref, core), (other_ref, 1 - core)))
-        ]
-
-    @pl.when(j == 0)
-    def _():
-        made = token_copies() + copies(0)
-        for copy in made + copies(1):
-            copy.start()
-        for copy in made:
-            copy.wait()
-
-    @pl.when(j == 1)
-    def _():
-        for copy in copies(1):
-            copy.wait()
-
-    out_ref[...] = jnp.dot(
-        tokens[...],
-        held[:, pl.ds(pl.multiple_of(j * tile, tile), tile)],
-        preferred_element_type=F32,
-    ).astype(BF)
-
-
-def weight_gradient(mine, other, blocks, hidden, first, count, before=None, tile=512):
-    features, rows = mine.shape[0], 2 * mine.shape[1]
+    for copy in copies:
+        copy.start()
+    for copy in copies:
+        copy.wait()
+
+
+def held_rows(blocks):
     pieces = [piece for block in blocks for piece in block]
     halves, number = [], 0
     for block in blocks:
@@ -297,25 +291,43 @@
         else:
             halves.append(((number, 0), (number + 1, 0)))
         number += len(block)
-    operands = [*pieces, mine, other]
-    aliases = {}
+    rows, hidden = len(blocks) * 128, pieces[0].shape[1]
+    return pl.pallas_call(
+        functools.partial(rows_kernel, tuple(halves)),
+        out_shape=pltpu.VMEM((rows, hidden), BF),
+        in_specs=[pl.BlockSpec(memory_space=pl.ANY)] * len(pieces),
+        out_specs=pl.BlockSpec(memory_space=pltpu.VMEM),
+        scratch_shapes=[pltpu.SemaphoreType.DMA((16,))],
+        compiler_params=params(52 * 1024 * 1024),
+        cost_estimate=cost(0, 4 * rows * hidden),
+        name="held_rows",
+    )(*pieces)
+
+
+def weight_kernel(tile, first, tokens, held, *refs):
+    columns = pl.ds(pl.multiple_of((first + pl.program_id(0)) * tile, tile), tile)
+    refs[-1][...] = jnp.dot(
+        tokens[...], held[:, columns], preferred_element_type=F32
+    ).astype(BF)
+
+
+def weight_gradient(tokens, held, first, count, before=None, tile=512):
+    features, rows = tokens.shape
+    hidden = held.shape[1]
+    operands, aliases = [tokens, held], {}
+    specs = [pl.BlockSpec(memory_space=pltpu.VMEM)] * 2
     if before is not None:
         aliases = {len(operands): 0}
         operands.append(before)
-    return pl.pallas_call(
-        functools.partial(weight_kernel, tile, first, count, tuple(halves)),
+        specs.append(pl.BlockSpec(memory_space=pl.ANY))
+    return pl.pallas_call(
+        functools.partial(weight_kernel, tile, first),
         out_shape=jax.ShapeDtypeStruct((features, hidden), BF),
         grid=(count,),
-        in_specs=[pl.BlockSpec(memory_space=pl.ANY)] * len(operands),
+        in_specs=specs,
         out_specs=pl.BlockSpec((features, tile), lambda j: (0, first + j)),
-        scratch_shapes=[
-            pltpu.VMEM((rows, count * tile), BF),
-            pltpu.VMEM((features, rows), BF),
-            pltpu.SemaphoreType.DMA((16, 2)),
-            pltpu.SemaphoreType.DMA((2,)),
-        ],
         input_output_aliases=aliases,
-        compiler_params=params(WHOLE),
+        compiler_params=params(LIMIT),
         cost_estimate=cost(3 * rows * features * count * tile, 2 * features * count * tile),
         name="weight_gradient",
     )(*operands)
@@ -323,7 +335,6 @@
 
 def local(tokens, weight, pre_act, upstream):
     y, z, x, h, core = place()
-    hidden = pre_act.shape[1]
 
     own = hidden_gradient(pre_act, upstream)
     up, down, across = row_shift(own, 1), row_shift(own, -1), row_shift(own, 0, 1)
@@ -346,18 +357,22 @@
     got1 = col_shift(send1, 0, 0, 1)
     own2, send2 = input_part([near[2], far[1], far[3]], weight)
     got2 = col_shift(send2, 0, 0, 1)
-    s0, s1, s2, s3 = dealt((((0, 0), (1, 1), (2, 3)), ((0, 2),)), [own1, got1, own2, got2], LIMIT)
+    s0, s1, s2, s3 = dealt(
+        ((own1, got1, 0), (own1, got1, 1), (own2, got2, 0), (own1, got1, 2)), LIMIT
+    )
     r1, r2, r3 = col_shift(s1, 1), col_shift(s2, 2), col_shift(s3, 3)
 
-    own3, send3 = input_part([(after(far_z[0], s1), far_z[1])], weight)
+    tokens_all = held_tokens(tokens_mine, tokens_other)
+    own3, send3 = input_part([(after(far_z[0], s1, tokens_all), far_z[1])], weight)
+    held = held_rows([(after(own, own3),), *near[1:], *far])
     got3 = after(col_shift(send3, 0, 0, 1), r1, r2, r3)
     t0, t1, t2, t3 = dealt(
-        (((3, 0),), ((1, 1), (2, 3)), ((0, 2),)), [own1, got1, own2, got2, own3, got3], WHOLE
+        ((own1, got1, 3), (own2, got2, 1), (own3, got3, 0), (own2, got2, 2)), WHOLE
     )
     v1, v2, v3 = col_shift(t1, 1), col_shift(t2, 2), col_shift(t3, 3)
 
-    tokens_other = after(tokens_other, t1)
-    weight_grad = weight_gradient(tokens_mine, tokens_other, near + far, hidden, 0, 4)
+    tokens_all = after(tokens_all, t1)
+    weight_grad = weight_gradient(tokens_all, held, 0, 4)
     t0, weight_grad = lax.optimization_barrier((t0, weight_grad))
 
     sum1 = s0 + r1.astype(F32) + r2.astype(F32) + r3.astype(F32)
@@ -366,9 +381,7 @@
     last = jnp.where(owner, sum2, sum1).astype(BF)
     last, weight_grad = lax.optimization_barrier((last, weight_grad))
     last = col_shift(last, 0, 1)
-    weight_grad = weight_gradient(
-        tokens_mine, tokens_other, near + far, hidden, 4, 2, weight_grad
-    )
+    weight_grad = weight_gradient(tokens_all, held, 4, 2, weight_grad)
     input_grad = (jnp.where(owner, sum1, sum2) + last.astype(F32)).astype(BF)
     return (input_grad, weight_grad)
 

time: 109 us -> 106 us (0.972)
  Pallas kernels: 43.2 us -> 38.8 us
  waiting for transfers between devices: 22.6 us -> 19.4 us
  other arithmetic: 2.03 us -> 4.26 us
  local copies, waits for them, and re-layouts: 7.51 us -> 9.36 us
    pallas_call x4 -> x6, Pallas kernels: 24.5 us -> 19.4 us  [the longest x2 13.2 us: weight_gradient(): pl.pallas_call(functools.partial(weight_kernel, tile, first), out_shape=j...]
    ppermute x8, waiting for transfers between devices: 15.9 us -> 11.1 us  [row_shift(): return lax.ppermute(value, 'row', pairs)]
    unnamed x44, local copies, waits for them, and re-layouts: 7.46 us -> 9.3 us
    ppermute x15, waiting for transfers between devices: 6.75 us -> 8.24 us  [col_shift(): return lax.ppermute(value, 'col', pairs)]
    convert_element_type x1, other arithmetic: 0.18 us -> 1.3 us  [local(): last = jnp.where(owner, sum2, sum1).astype(BF)]
    convert_element_type x1, other arithmetic: 0.88 us -> 2 us  [local(): input_grad = (jnp.where(owner, sum1, sum2) + last.astype(F32)).astype(BF)]
  transfers between devices with their start and end apart: 23 -> 23, of which waited for: 6 -> 8; matrix products, arithmetic and copies ran while one was open for 1% -> 1% of each run, Pallas kernels for 39% -> 34%
where the time goes in v3:
time: 106 us
  Pallas kernels  38.8 us (37%)
  starting transfers between devices  33.1 us (31%)
  waiting for transfers between devices  19.4 us (18%)
  local copies, waits for them, and re-layouts  9.36 us (9%)
  other arithmetic  4.26 us (4%)
    ppermute x15, starting transfers between devices, col_shift(): return lax.ppermute(value, 'col', pairs)  22.5 us
    pallas_call x3, Pallas kernels, input_part(): pl.pallas_call(functools.partial(input_kernel, layout), out_shape=(jax.Sh...  14.9 us
    pallas_call x2, Pallas kernels, weight_gradient(): pl.pallas_call(functools.partial(weight_kernel, tile, first), out_shape=j...  13.2 us
    ppermute x8, waiting for transfers between devices, row_shift(): return lax.ppermute(value, 'row', pairs)  11.1 us
    ppermute x8, starting transfers between devices, row_shift(): return lax.ppermute(value, 'row', pairs)  10.6 us
    unnamed x44, local copies, waits for them, and re-layouts  9.3 us
    ppermute x15, waiting for transfers between devices, col_shift(): return lax.ppermute(value, 'col', pairs)  8.24 us
    pallas_call x1, Pallas kernels, held_rows(): pl.pallas_call(functools.partial(rows_kernel, tuple(halves)), out_shape=p...  3 us
  transfers between devices with their start and end apart: 23, of which 8 were waited for; matrix products, arithmetic and copies ran while one was open for 1% of the time, Pallas kernels for 34%

profile of v3, /device:TPU:0, one launch (start us, length us, event | category | flops | bytes accessed | tf_op | source)
XLA Modules:
  0.0 105.9 jit_solution(3258980679997610315)
XLA Ops:
  4.2 3.2 %collective-permute-start = (bf16[128,3072]{1,0:T(8,128)(2,1)S(1)}, bf16[128,3072]{1,0:T(8,128)(2,1)S(1)}, u32[]{:S(2)}, u32[]{:S(2)}) collective-permute-start(bf16[128,3072]{1,0:T(8,128)(2,1)S(1)} %hidden_gradient.1.refs_0_), channel_id=1, source_target_pairs={{0,96},{16,112},{32,0},{48,16},{64,32},{80,48},{96,64},{112,80},{1... | collective-permute-start | bytes 2359304 | tf_op jit(solution)/shard_map/ppermute | solution.py:33
  7.3 3.9 %collective-permute-start.12 = (bf16[64,1536]{1,0:T(8,128)(2,1)}, bf16[64,1536]{1,0:T(8,128)(2,1)S(1)}, u32[]{:S(2)}, u32[]{:S(2)}) collective-permute-start(bf16[64,1536]{1,0:T(8,128)(2,1)} %param.4), channel_id=1, source_target_pairs={{0,2},{1,3},{2,0},{3,1},{4,6},{5,7},{6,4},{7,5},{8,10},{9,11},{10,... | collective-permute-start | bytes 589832 | tf_op jit(solution)/shard_map/ppermute | solution.py:43
  12.2 5.0 %collective-permute-done.12 = bf16[64,1536]{1,0:T(8,128)(2,1)S(1)} collective-permute-done((bf16[64,1536]{1,0:T(8,128)(2,1)}, bf16[64,1536]{1,0:T(8,128)(2,1)S(1)}, u32[]{:S(2)}, u32[]{:S(2)}) %collective-permute-start.12) | collective-permute-done | bytes 196640 | tf_op jit(solution)/shard_map/ppermute | solution.py:43
  18.2 1.6 %collective-permute-start.13 = (bf16[2,64,1536]{2,1,0:T(8,128)(2,1)S(1)}, bf16[2,64,1536]{2,1,0:T(8,128)(2,1)S(1)}, u32[]{:S(2)}, u32[]{:S(2)}) collective-permute-start(bf16[2,64,1536]{2,1,0:T(8,128)(2,1)S(1)} %pad_maximum_fusion.refs_0_), channel_id=1, source_target_pairs={{0,4},{1,5},{2,6},{3,7},{4,8},{5,9},{6,10},{7,11},{8,12},{9,13},{1... | collective-permute-start | bytes 1179656 | tf_op jit(solution)/shard_map/ppermute | solution.py:43
  19.7 2.7 %collective-permute-start.14 = (bf16[2,64,1536]{2,1,0:T(8,128)(2,1)S(1)}, bf16[2,64,1536]{2,1,0:T(8,128)(2,1)S(1)}, u32[]{:S(2)}, u32[]{:S(2)}) collective-permute-start(bf16[2,64,1536]{2,1,0:T(8,128)(2,1)S(1)} %pad_maximum_fusion.refs_0_), channel_id=1, source_target_pairs={{0,8},{1,9},{2,10},{3,11},{4,12},{5,13},{6,14},{7,15},{8,0},{9,1},... | collective-permute-start | bytes 1179656 | tf_op jit(solution)/shard_map/ppermute | solution.py:43
  22.4 1.7 %collective-permute-done.refs_1_ = bf16[128,3072]{1,0:T(8,128)(2,1)S(1)} collective-permute-done((bf16[128,3072]{1,0:T(8,128)(2,1)S(1)}, bf16[128,3072]{1,0:T(8,128)(2,1)S(1)}, u32[]{:S(2)}, u32[]{:S(2)}) %collective-permute-start) | collective-permute-done | bytes 786464 | tf_op jit(solution)/shard_map/ppermute | solution.py:33
  24.1 2.8 %collective-permute-start.15 = (bf16[2,64,1536]{2,1,0:T(8,128)(2,1)S(1)}, bf16[2,64,1536]{2,1,0:T(8,128)(2,1)S(1)}, u32[]{:S(2)}, u32[]{:S(2)}) collective-permute-start(bf16[2,64,1536]{2,1,0:T(8,128)(2,1)S(1)} %pad_maximum_fusion.refs_0_), channel_id=1, source_target_pairs={{0,12},{1,13},{2,14},{3,15},{4,0},{5,1},{6,2},{7,3},{8,4},{9,5},{1... | collective-permute-start | bytes 1179656 | tf_op jit(solution)/shard_map/ppermute | solution.py:43
  26.9 6.7 %collective-permute-done.2.refs_3_.refs_4_ = bf16[128,3072]{1,0:T(8,128)(2,1)S(1)} collective-permute-done((bf16[128,3072]{1,0:T(8,128)(2,1)S(1)}, bf16[128,3072]{1,0:T(8,128)(2,1)S(1)}, u32[]{:S(2)}, u32[]{:S(2)}) %collective-permute-start.2) | collective-permute-done | bytes 786464 | tf_op jit(solution)/shard_map/ppermute | solution.py:33
  37.7 2.6 %transposed_tokens.1.mine_ref = bf16[1536,512]{1,0:T(8,128)(2,1)S(1)} custom-call(bf16[2,64,1536]{2,1,0:T(8,128)(2,1)S(1)} %pad_maximum_fusion.refs_0_, bf16[2,64,1536]{2,1,0:T(8,128)(2,1)S(1)} %collective-permute-done.13.refs_1_, bf16[2,64,1536]{2,1,0:T(8,128)(2,1)S(1)} %collective-permute-done.14.refs_2_, ...), custom_call_target="tpu_custom_call" | custom-call | bytes 6291456 | tf_op jit(solution)/shard_map/transposed_tokens/pallas_call | solution.py:102
  40.4 3.7 %copy-done.2 = bf16[1536,3072]{1,0:T(8,128)(2,1)S(1)} copy-done((bf16[1536,3072]{1,0:T(8,128)(2,1)S(1)}, bf16[1536,3072]{1,0:T(8,128)(2,1)}, u32[]{:S(2)}) %copy-start.2) | copy-done | bytes 9437208
  44.7 5.9 %input_part.3 = (f32[4,64,1536]{2,1,0:T(8,128)S(1)}, bf16[4,64,1536]{2,1,0:T(8,128)(2,1)S(1)}) custom-call(bf16[128,3072]{1,0:T(8,128)(2,1)S(1)} %hidden_gradient.1.refs_0_, bf16[128,3072]{1,0:T(8,128)(2,1)S(1)} %collective-permute-done.refs_1_, bf16[128,3072]{1,0:T(8,128)(2,1)S(1)} %collective-permute-done.1.refs_2_.refs_3_, ...), custom_call_target="tpu_custom_call" | custom-call | flops 4831838208 | bytes 12582912 | tf_op jit(solution)/shard_map/input_part/pallas_call | solution.py:212
  51.3 2.2 %collective-permute-done.4.refs_0_.refs_2_ = bf16[128,3072]{1,0:T(8,128)(2,1)S(1)} collective-permute-done((bf16[128,3072]{1,0:T(8,128)(2,1)S(1)}, bf16[128,3072]{1,0:T(8,128)(2,1)S(1)}, u32[]{:S(2)}, u32[]{:S(2)}) %collective-permute-start.4) | collective-permute-done | bytes 786464 | tf_op jit(solution)/shard_map/ppermute | solution.py:33
  53.4 4.5 %input_part.4 = (f32[3,64,1536]{2,1,0:T(8,128)S(1)}, bf16[3,64,1536]{2,1,0:T(8,128)(2,1)S(1)}) custom-call(bf16[128,3072]{1,0:T(8,128)(2,1)S(1)} %collective-permute-done.4.refs_0_.refs_2_, bf16[128,3072]{1,0:T(8,128)(2,1)S(1)} %collective-permute-done.5.refs_1_.refs_5_, bf16[128,3072]{1,0:T(8,128)(2,1)S(1)} %collective-permute-done.6.refs_2_.refs_8_, ...), custom_call_target="tpu_custom_call" | custom-call | flops 3623878656 | bytes 11796480 | tf_op jit(solution)/shard_map/input_part/pallas_call | solution.py:212
  58.3 3.2 %collective-permute-start.17 = (bf16[64,3072]{1,0:T(8,128)(2,1)S(1)}, bf16[64,3072]{1,0:T(8,128)(2,1)S(1)}, u32[]{:S(2)}, u32[]{:S(2)}) collective-permute-start(bf16[64,3072]{1,0:T(8,128)(2,1)S(1)} %slice.9), channel_id=1, source_target_pairs={{0,96},{16,112},{32,0},{48,16},{64,32},{80,48},{96,64},{112,80},{1... | collective-permute-start | bytes 1179656 | tf_op jit(solution)/shard_map/ppermute | solution.py:33
  62.8 2.8 %collective-permute-start.10 = (bf16[64,1536]{1,0:T(8,128)(2,1)}, bf16[64,1536]{1,0:T(8,128)(2,1)}, u32[]{:S(2)}, u32[]{:S(2)}) collective-permute-start(bf16[64,1536]{1,0:T(8,128)(2,1)} %get-tuple-element.35), channel_id=1, source_target_pairs={{0,12},{1,13},{2,14},{3,15},{4,0},{5,1},{6,2},{7,3},{8,4},{9,5},{1... | collective-permute-start | bytes 589832 | tf_op jit(solution)/shard_map/ppermute | solution.py:43
  70.9 4.5 %input_part.5 = (f32[1,64,1536]{2,1,0:T(8,128)S(1)}, bf16[1,64,1536]{2,1,0:T(8,128)(2,1)}) custom-call(bf16[64,3072]{1,0:T(8,128)(2,1)S(1)} %collective-permute-done.11.refs_0_.refs_6_, bf16[64,3072]{1,0:T(8,128)(2,1)S(1)} %collective-permute-done.17.refs_1_.refs_7_, bf16[1536,3072]{1,0:T(8,128)(2,1)S(1)} %held_weight.1.refs_4_.refs_3_.refs_2_), custom_call_target="tpu_custom_call" | custom-call | flops 1207959552 | bytes 10223616 | tf_op jit(solution)/shard_map/input_part/pallas_call | solution.py:212
  76.2 3.0 %held_rows.1.held = bf16[1024,3072]{1,0:T(8,128)(2,1)S(1)} custom-call(bf16[128,3072]{1,0:T(8,128)(2,1)} %copy-done.5, bf16[128,3072]{1,0:T(8,128)(2,1)} %copy-done.14, bf16[128,3072]{1,0:T(8,128)(2,1)} %copy-done.17, bf16[128,3072]{1,0:T(8,128)(2,1)} %copy-done.16, bf16[128,3072]{1,0:T(8,128)(2,1)} %copy-done.15, bf16[128,3072]{1,0:T(8,128)(2,1)} %copy-done.6, ...), custom_call_target="tpu_custom_call" | custom-call | bytes 12582912 | tf_op jit(solution)/shard_map/held_rows/pallas_call | solution.py:295
  80.8 1.6 %collective-permute-start.19 = (bf16[64,1536]{1,0:T(8,128)(2,1)S(1)}, bf16[64,1536]{1,0:T(8,128)(2,1)S(1)}, u32[]{:S(2)}, u32[]{:S(2)}) collective-permute-start(bf16[64,1536]{1,0:T(8,128)(2,1)S(1)} %get-tuple-element.41), channel_id=1, source_target_pairs={{0,4},{1,5},{2,6},{3,7},{4,8},{5,9},{6,10},{7,11},{8,12},{9,13},{1... | collective-permute-start | bytes 589832 | tf_op jit(solution)/shard_map/ppermute | solution.py:43
  82.4 1.7 %collective-permute-start.21 = (bf16[64,1536]{1,0:T(8,128)(2,1)S(1)}, bf16[64,1536]{1,0:T(8,128)(2,1)S(1)}, u32[]{:S(2)}, u32[]{:S(2)}) collective-permute-start(bf16[64,1536]{1,0:T(8,128)(2,1)S(1)} %get-tuple-element.46), channel_id=1, source_target_pairs={{0,12},{1,13},{2,14},{3,15},{4,0},{5,1},{6,2},{7,3},{8,4},{9,5},{1... | collective-permute-start | bytes 589832 | tf_op jit(solution)/shard_map/ppermute | solution.py:43
  84.1 1.8 %collective-permute-start.20 = (bf16[64,1536]{1,0:T(8,128)(2,1)S(1)}, bf16[64,1536]{1,0:T(8,128)(2,1)S(1)}, u32[]{:S(2)}, u32[]{:S(2)}) collective-permute-start(bf16[64,1536]{1,0:T(8,128)(2,1)S(1)} %get-tuple-element.45), channel_id=1, source_target_pairs={{0,8},{1,9},{2,10},{3,11},{4,12},{5,13},{6,14},{7,15},{8,0},{9,1},... | collective-permute-start | bytes 589832 | tf_op jit(solution)/shard_map/ppermute | solution.py:43
  85.9 8.4 %weight_gradient.2.refs_0_ = bf16[1536,3072]{1,0:T(8,128)(2,1)} custom-call(bf16[1536,1024]{1,0:T(8,128)(2,1)S(1)} %copy-done.1, bf16[1024,3072]{1,0:T(8,128)(2,1)S(1)} %held_rows.1.held), custom_call_target="tpu_custom_call" | custom-call | flops 9663676416 | bytes 6291456 | tf_op jit(solution)/shard_map/weight_gradient/pallas_call | solution.py:323
  97.1 4.8 %weight_gradient.3 = bf16[1536,3072]{1,0:T(8,128)(2,1)} custom-call(bf16[1536,1024]{1,0:T(8,128)(2,1)S(1)} %copy-done.1, bf16[1024,3072]{1,0:T(8,128)(2,1)S(1)} %held_rows.1.held, bf16[1536,3072]{1,0:T(8,128)(2,1)} %weight_gradient.2.refs_0_), custom_call_target="tpu_custom_call", output_to_operand_aliasing={{}: (2, {})} | custom-call | flops 4831838208 | bytes 3145728 | tf_op jit(solution)/shard_map/weight_gradient/pallas_call | solution.py:323
  101.8 2.0 %collective-permute-done.22 = bf16[64,1536]{1,0:T(8,128)(2,1)S(1)} collective-permute-done((bf16[64,1536]{1,0:T(8,128)(2,1)S(1)}, bf16[64,1536]{1,0:T(8,128)(2,1)S(1)}, u32[]{:S(2)}, u32[]{:S(2)}) %collective-permute-start.22) | collective-permute-done | bytes 196640 | tf_op jit(solution)/shard_map/ppermute | solution.py:43
  103.9 2.0 %add_convert_fusion = bf16[64,1536]{1,0:T(8,128)(2,1)} fusion(bf16[64,1536]{1,0:T(8,128)(2,1)S(1)} %collective-permute-done.22, pred[]{:T(512)S(6)} %eq.6, bf16[64,1536]{1,0:T(8,128)(2,1)} %collective-permute-done.10, bf16[64,1536]{1,0:T(8,128)(2,1)} %collective-permute-done.9, f32[64,1536]{1,0:T(8,128)S(1)} %copy-done.11, ...), kind=kLoop, calls=%fused_computation.1 | loop fusion | flops 1572864 | bytes 2359297 | tf_op jit(solution)/shard_map/convert_element_type | solution.py:385
  (83 shorter events, 22.9 us)
Async XLA Ops:
  4.2 40.5 %copy-start.5 = (bf16[128,3072]{1,0:T(8,128)(2,1)}, bf16[128,3072]{1,0:T(8,128)(2,1)S(1)}, u32[]{:S(2)}) copy-start(bf16[128,3072]{1,0:T(8,128)(2,1)S(1)} %hidden_gradient.1.refs_0_) | copy-start | bytes 2359300
  4.2 20.0 %collective-permute-start = (bf16[128,3072]{1,0:T(8,128)(2,1)S(1)}, bf16[128,3072]{1,0:T(8,128)(2,1)S(1)}, u32[]{:S(2)}, u32[]{:S(2)}) collective-permute-start(bf16[128,3072]{1,0:T(8,128)(2,1)S(1)} %hidden_gradient.1.refs_0_), channel_id=1, source_target_pairs={{0,96},{16,112},{32,0},{48,16},{64,32},{80,48},{96,64},{112,80},{1... | collective-permute-start | bytes 2359304 | tf_op jit(solution)/shard_map/ppermute | solution.py:33
  7.3 9.9 %collective-permute-start.12 = (bf16[64,1536]{1,0:T(8,128)(2,1)}, bf16[64,1536]{1,0:T(8,128)(2,1)S(1)}, u32[]{:S(2)}, u32[]{:S(2)}) collective-permute-start(bf16[64,1536]{1,0:T(8,128)(2,1)} %param.4), channel_id=1, source_target_pairs={{0,2},{1,3},{2,0},{3,1},{4,6},{5,7},{6,4},{7,5},{8,10},{9,11},{10,... | collective-permute-start | bytes 589832 | tf_op jit(solution)/shard_map/ppermute | solution.py:43
  11.2 22.4 %collective-permute-start.2 = (bf16[128,3072]{1,0:T(8,128)(2,1)S(1)}, bf16[128,3072]{1,0:T(8,128)(2,1)S(1)}, u32[]{:S(2)}, u32[]{:S(2)}) collective-permute-start(bf16[128,3072]{1,0:T(8,128)(2,1)S(1)} %hidden_gradient.1.refs_0_), channel_id=1, source_target_pairs={{0,16},{16,0},{32,48},{48,32},{64,80},{80,64},{96,112},{112,96},{1... | collective-permute-start | bytes 2359304 | tf_op jit(solution)/shard_map/ppermute | solution.py:33
  12.2 22.1 %collective-permute-start.1 = (bf16[128,3072]{1,0:T(8,128)(2,1)S(1)}, bf16[128,3072]{1,0:T(8,128)(2,1)S(1)}, u32[]{:S(2)}, u32[]{:S(2)}) collective-permute-start(bf16[128,3072]{1,0:T(8,128)(2,1)S(1)} %hidden_gradient.1.refs_0_), channel_id=1, source_target_pairs={{0,32},{16,48},{32,64},{48,80},{64,96},{80,112},{96,0},{112,16},{1... | collective-permute-start | bytes 2359304 | tf_op jit(solution)/shard_map/ppermute | solution.py:33
  18.2 17.5 %collective-permute-start.13 = (bf16[2,64,1536]{2,1,0:T(8,128)(2,1)S(1)}, bf16[2,64,1536]{2,1,0:T(8,128)(2,1)S(1)}, u32[]{:S(2)}, u32[]{:S(2)}) collective-permute-start(bf16[2,64,1536]{2,1,0:T(8,128)(2,1)S(1)} %pad_maximum_fusion.refs_0_), channel_id=1, source_target_pairs={{0,4},{1,5},{2,6},{3,7},{4,8},{5,9},{6,10},{7,11},{8,12},{9,13},{1... | collective-permute-start | bytes 1179656 | tf_op jit(solution)/shard_map/ppermute | solution.py:43
  19.7 18.0 %collective-permute-start.14 = (bf16[2,64,1536]{2,1,0:T(8,128)(2,1)S(1)}, bf16[2,64,1536]{2,1,0:T(8,128)(2,1)S(1)}, u32[]{:S(2)}, u32[]{:S(2)}) collective-permute-start(bf16[2,64,1536]{2,1,0:T(8,128)(2,1)S(1)} %pad_maximum_fusion.refs_0_), channel_id=1, source_target_pairs={{0,8},{1,9},{2,10},{3,11},{4,12},{5,13},{6,14},{7,15},{8,0},{9,1},... | collective-permute-start | bytes 1179656 | tf_op jit(solution)/shard_map/ppermute | solution.py:43
  24.1 13.5 %collective-permute-start.15 = (bf16[2,64,1536]{2,1,0:T(8,128)(2,1)S(1)}, bf16[2,64,1536]{2,1,0:T(8,128)(2,1)S(1)}, u32[]{:S(2)}, u32[]{:S(2)}) collective-permute-start(bf16[2,64,1536]{2,1,0:T(8,128)(2,1)S(1)} %pad_maximum_fusion.refs_0_), channel_id=1, source_target_pairs={{0,12},{1,13},{2,14},{3,15},{4,0},{5,1},{6,2},{7,3},{8,4},{9,5},{1... | collective-permute-start | bytes 1179656 | tf_op jit(solution)/shard_map/ppermute | solution.py:43
  33.6 19.8 %collective-permute-start.5 = (bf16[128,3072]{1,0:T(8,128)(2,1)S(1)}, bf16[128,3072]{1,0:T(8,128)(2,1)S(1)}, u32[]{:S(2)}, u32[]{:S(2)}) collective-permute-start(bf16[128,3072]{1,0:T(8,128)(2,1)S(1)} %collective-permute-done.2.refs_3_.refs_4_), channel_id=1, source_target_pairs={{0,96},{16,112},{32,0},{48,16},{64,32},{80,48},{96,64},{112,80},{1... | collective-permute-start | bytes 2359304 | tf_op jit(solution)/shard_map/ppermute | solution.py:33
  34.4 19.0 %collective-permute-start.4 = (bf16[128,3072]{1,0:T(8,128)(2,1)S(1)}, bf16[128,3072]{1,0:T(8,128)(2,1)S(1)}, u32[]{:S(2)}, u32[]{:S(2)}) collective-permute-start(bf16[128,3072]{1,0:T(8,128)(2,1)S(1)} %collective-permute-done.1.refs_2_.refs_3_), channel_id=1, source_target_pairs={{0,32},{16,48},{32,64},{48,80},{64,96},{80,112},{96,0},{112,16},{1... | collective-permute-start | bytes 2359304 | tf_op jit(solution)/shard_map/ppermute | solution.py:33
  35.7 17.7 %collective-permute-start.6 = (bf16[128,3072]{1,0:T(8,128)(2,1)S(1)}, bf16[128,3072]{1,0:T(8,128)(2,1)S(1)}, u32[]{:S(2)}, u32[]{:S(2)}) collective-permute-start(bf16[128,3072]{1,0:T(8,128)(2,1)S(1)} %collective-permute-done.1.refs_2_.refs_3_), channel_id=1, source_target_pairs={{0,16},{16,0},{32,48},{48,32},{64,80},{80,64},{96,112},{112,96},{1... | collective-permute-start | bytes 2359304 | tf_op jit(solution)/shard_map/ppermute | solution.py:33
  40.3 26.1 %collective-permute-start.16 = (bf16[1536,512]{1,0:T(8,128)(2,1)S(1)}, bf16[1536,512]{1,0:T(8,128)(2,1)S(1)}, u32[]{:S(2)}, u32[]{:S(2)}) collective-permute-start(bf16[1536,512]{1,0:T(8,128)(2,1)S(1)} %transposed_tokens.1.mine_ref), channel_id=1, source_target_pairs={{0,1},{1,0},{2,3},{3,2},{4,5},{5,4},{6,7},{7,6},{8,9},{9,8},{10,11... | collective-permute-start | bytes 4718600 | tf_op jit(solution)/shard_map/ppermute | solution.py:43
  50.6 10.9 %collective-permute-start.3 = (bf16[4,64,1536]{2,1,0:T(8,128)(2,1)S(1)}, bf16[4,64,1536]{2,1,0:T(8,128)(2,1)S(1)}, u32[]{:S(2)}, u32[]{:S(2)}) collective-permute-start(bf16[4,64,1536]{2,1,0:T(8,128)(2,1)S(1)} %get-tuple-element.27), channel_id=1, source_target_pairs={{0,1},{1,0},{2,3},{3,2},{4,5},{5,4},{6,7},{7,6},{8,9},{9,8},{10,11... | collective-permute-start | bytes 2359304 | tf_op jit(solution)/shard_map/ppermute | solution.py:43
  58.0 3.6 %collective-permute-start.7 = (bf16[3,64,1536]{2,1,0:T(8,128)(2,1)S(1)}, bf16[3,64,1536]{2,1,0:T(8,128)(2,1)S(1)}, u32[]{:S(2)}, u32[]{:S(2)}) collective-permute-start(bf16[3,64,1536]{2,1,0:T(8,128)(2,1)S(1)} %get-tuple-element.31), channel_id=1, source_target_pairs={{0,1},{1,0},{2,3},{3,2},{4,5},{5,4},{6,7},{7,6},{8,9},{9,8},{10,11... | collective-permute-start | bytes 1769480 | tf_op jit(solution)/shard_map/ppermute | solution.py:43
  58.1 12.8 %collective-permute-start.11 = (bf16[64,3072]{1,0:T(8,128)(2,1)S(1)}, bf16[64,3072]{1,0:T(8,128)(2,1)S(1)}, u32[]{:S(2)}, u32[]{:S(2)}) collective-permute-start(bf16[64,3072]{1,0:T(8,128)(2,1)S(1)} %slice.8), channel_id=1, source_target_pairs={{0,32},{16,48},{32,64},{48,80},{64,96},{80,112},{96,0},{112,16},{1... | collective-permute-start | bytes 1179656 | tf_op jit(solution)/shard_map/ppermute | solution.py:33
  58.3 12.6 %collective-permute-start.17 = (bf16[64,3072]{1,0:T(8,128)(2,1)S(1)}, bf16[64,3072]{1,0:T(8,128)(2,1)S(1)}, u32[]{:S(2)}, u32[]{:S(2)}) collective-permute-start(bf16[64,3072]{1,0:T(8,128)(2,1)S(1)} %slice.9), channel_id=1, source_target_pairs={{0,96},{16,112},{32,0},{48,16},{64,32},{80,48},{96,64},{112,80},{1... | collective-permute-start | bytes 1179656 | tf_op jit(solution)/shard_map/ppermute | solution.py:33
  62.8 16.5 %collective-permute-start.10 = (bf16[64,1536]{1,0:T(8,128)(2,1)}, bf16[64,1536]{1,0:T(8,128)(2,1)}, u32[]{:S(2)}, u32[]{:S(2)}) collective-permute-start(bf16[64,1536]{1,0:T(8,128)(2,1)} %get-tuple-element.35), channel_id=1, source_target_pairs={{0,12},{1,13},{2,14},{3,15},{4,0},{5,1},{6,2},{7,3},{8,4},{9,5},{1... | collective-permute-start | bytes 589832 | tf_op jit(solution)/shard_map/ppermute | solution.py:43
  65.6 13.7 %collective-permute-start.9 = (bf16[64,1536]{1,0:T(8,128)(2,1)}, bf16[64,1536]{1,0:T(8,128)(2,1)}, u32[]{:S(2)}, u32[]{:S(2)}) collective-permute-start(bf16[64,1536]{1,0:T(8,128)(2,1)} %get-tuple-element.34), channel_id=1, source_target_pairs={{0,8},{1,9},{2,10},{3,11},{4,12},{5,13},{6,14},{7,15},{8,0},{9,1},... | collective-permute-start | bytes 589832 | tf_op jit(solution)/shard_map/ppermute | solution.py:43
  67.5 11.8 %collective-permute-start.8 = (bf16[64,1536]{1,0:T(8,128)(2,1)}, bf16[64,1536]{1,0:T(8,128)(2,1)}, u32[]{:S(2)}, u32[]{:S(2)}) collective-permute-start(bf16[64,1536]{1,0:T(8,128)(2,1)} %get-tuple-element.33), channel_id=1, source_target_pairs={{0,4},{1,5},{2,6},{3,7},{4,8},{5,9},{6,10},{7,11},{8,12},{9,13},{1... | collective-permute-start | bytes 589832 | tf_op jit(solution)/shard_map/ppermute | solution.py:43
  76.2 3.1 %collective-permute-start.18 = (bf16[1,64,1536]{2,1,0:T(8,128)(2,1)}, bf16[1,64,1536]{2,1,0:T(8,128)(2,1)}, u32[]{:S(2)}, u32[]{:S(2)}) collective-permute-start(bf16[1,64,1536]{2,1,0:T(8,128)(2,1)} %get-tuple-element.38), channel_id=1, source_target_pairs={{0,1},{1,0},{2,3},{3,2},{4,5},{5,4},{6,7},{7,6},{8,9},{9,8},{10,11... | collective-permute-start | bytes 589832 | tf_op jit(solution)/shard_map/ppermute | solution.py:43
  80.8 13.7 %collective-permute-start.19 = (bf16[64,1536]{1,0:T(8,128)(2,1)S(1)}, bf16[64,1536]{1,0:T(8,128)(2,1)S(1)}, u32[]{:S(2)}, u32[]{:S(2)}) collective-permute-start(bf16[64,1536]{1,0:T(8,128)(2,1)S(1)} %get-tuple-element.41), channel_id=1, source_target_pairs={{0,4},{1,5},{2,6},{3,7},{4,8},{5,9},{6,10},{7,11},{8,12},{9,13},{1... | collective-permute-start | bytes 589832 | tf_op jit(solution)/shard_map/ppermute | solution.py:43
  82.4 12.0 %collective-permute-start.21 = (bf16[64,1536]{1,0:T(8,128)(2,1)S(1)}, bf16[64,1536]{1,0:T(8,128)(2,1)S(1)}, u32[]{:S(2)}, u32[]{:S(2)}) collective-permute-start(bf16[64,1536]{1,0:T(8,128)(2,1)S(1)} %get-tuple-element.46), channel_id=1, source_target_pairs={{0,12},{1,13},{2,14},{3,15},{4,0},{5,1},{6,2},{7,3},{8,4},{9,5},{1... | collective-permute-start | bytes 589832 | tf_op jit(solution)/shard_map/ppermute | solution.py:43
  84.1 10.4 %collective-permute-start.20 = (bf16[64,1536]{1,0:T(8,128)(2,1)S(1)}, bf16[64,1536]{1,0:T(8,128)(2,1)S(1)}, u32[]{:S(2)}, u32[]{:S(2)}) collective-permute-start(bf16[64,1536]{1,0:T(8,128)(2,1)S(1)} %get-tuple-element.45), channel_id=1, source_target_pairs={{0,8},{1,9},{2,10},{3,11},{4,12},{5,13},{6,14},{7,15},{8,0},{9,1},... | collective-permute-start | bytes 589832 | tf_op jit(solution)/shard_map/ppermute | solution.py:43
  95.8 8.1 %collective-permute-start.22 = (bf16[64,1536]{1,0:T(8,128)(2,1)S(1)}, bf16[64,1536]{1,0:T(8,128)(2,1)S(1)}, u32[]{:S(2)}, u32[]{:S(2)}) collective-permute-start(bf16[64,1536]{1,0:T(8,128)(2,1)S(1)} %select_convert_fusion), channel_id=1, source_target_pairs={{0,2},{1,3},{2,0},{3,1},{4,6},{5,7},{6,4},{7,5},{8,10},{9,11},{10,... | collective-permute-start | bytes 589832 | tf_op jit(solution)/shard_map/ppermute | solution.py:43
  (21 other events, 125.7 us)

commit v4 on v3

--- a/solution.py
+++ b/solution.py
@@ -382,7 +382,8 @@
     last, weight_grad = lax.optimization_barrier((last, weight_grad))
     last = col_shift(last, 0, 1)
     weight_grad = weight_gradient(tokens_all, held, 4, 2, weight_grad)
-    input_grad = (jnp.where(owner, sum1, sum2) + last.astype(F32)).astype(BF)
+    kept = lax.optimization_barrier(jnp.where(owner, sum1, sum2))
+    input_grad = (kept + last.astype(F32)).astype(BF)
     return (input_grad, weight_grad)
 
 

time: 106 us -> 105 us (level)
  other arithmetic: 4.26 us -> 2.98 us
    convert_element_type x1, other arithmetic: 2 us -> 0.71 us  [local(): input_grad = (kept + last.astype(F32)).astype(BF)]
  transfers between devices with their start and end apart: 23 -> 23, of which waited for: 8 -> 7; matrix products, arithmetic and copies ran while one was open for 1% -> 1% of each run, Pallas kernels for 34% -> 35%
where the time goes in v4:
time: 105 us
  Pallas kernels  38.8 us (37%)
  starting transfers between devices  32.9 us (31%)
  waiting for transfers between devices  18.8 us (18%)
  local copies, waits for them, and re-layouts  10.1 us (10%)
  other arithmetic  2.98 us (3%)
    ppermute x15, starting transfers between devices, col_shift(): return lax.ppermute(value, 'col', pairs)  22.3 us
    pallas_call x3, Pallas kernels, input_part(): pl.pallas_call(functools.partial(input_kernel, layout), out_shape=(jax.Sh...  14.9 us
    pallas_call x2, Pallas kernels, weight_gradient(): pl.pallas_call(functools.partial(weight_kernel, tile, first), out_shape=j...  13.2 us
    ppermute x8, starting transfers between devices, row_shift(): return lax.ppermute(value, 'row', pairs)  10.6 us
    ppermute x8, waiting for transfers between devices, row_shift(): return lax.ppermute(value, 'row', pairs)  10.6 us
    unnamed x44, local copies, waits for them, and re-layouts  10.1 us
    ppermute x15, waiting for transfers between devices, col_shift(): return lax.ppermute(value, 'col', pairs)  8.18 us
    pallas_call x1, Pallas kernels, held_rows(): pl.pallas_call(functools.partial(rows_kernel, tuple(halves)), out_shape=p...  3 us
  transfers between devices with their start and end apart: 23, of which 7 were waited for; matrix products, arithmetic and copies ran while one was open for 1% of the time, Pallas kernels for 35%

profile of v4, /device:TPU:0, one launch (start us, length us, event | category | flops | bytes accessed | tf_op | source)
XLA Modules:
  0.0 104.6 jit_solution(17467417214318695032)
XLA Ops:
  4.2 3.2 %collective-permute-start = (bf16[128,3072]{1,0:T(8,128)(2,1)S(1)}, bf16[128,3072]{1,0:T(8,128)(2,1)S(1)}, u32[]{:S(2)}, u32[]{:S(2)}) collective-permute-start(bf16[128,3072]{1,0:T(8,128)(2,1)S(1)} %hidden_gradient.1.refs_0_), channel_id=1, source_target_pairs={{0,96},{16,112},{32,0},{48,16},{64,32},{80,48},{96,64},{112,80},{1... | collective-permute-start | bytes 2359304 | tf_op jit(solution)/shard_map/ppermute | solution.py:33
  7.3 3.9 %collective-permute-start.12 = (bf16[64,1536]{1,0:T(8,128)(2,1)}, bf16[64,1536]{1,0:T(8,128)(2,1)S(1)}, u32[]{:S(2)}, u32[]{:S(2)}) collective-permute-start(bf16[64,1536]{1,0:T(8,128)(2,1)} %param.4), channel_id=1, source_target_pairs={{0,2},{1,3},{2,0},{3,1},{4,6},{5,7},{6,4},{7,5},{8,10},{9,11},{10,... | collective-permute-start | bytes 589832 | tf_op jit(solution)/shard_map/ppermute | solution.py:43
  12.2 5.0 %collective-permute-done.12 = bf16[64,1536]{1,0:T(8,128)(2,1)S(1)} collective-permute-done((bf16[64,1536]{1,0:T(8,128)(2,1)}, bf16[64,1536]{1,0:T(8,128)(2,1)S(1)}, u32[]{:S(2)}, u32[]{:S(2)}) %collective-permute-start.12) | collective-permute-done | bytes 196640 | tf_op jit(solution)/shard_map/ppermute | solution.py:43
  18.2 1.6 %collective-permute-start.13 = (bf16[2,64,1536]{2,1,0:T(8,128)(2,1)S(1)}, bf16[2,64,1536]{2,1,0:T(8,128)(2,1)S(1)}, u32[]{:S(2)}, u32[]{:S(2)}) collective-permute-start(bf16[2,64,1536]{2,1,0:T(8,128)(2,1)S(1)} %pad_maximum_fusion.refs_0_), channel_id=1, source_target_pairs={{0,4},{1,5},{2,6},{3,7},{4,8},{5,9},{6,10},{7,11},{8,12},{9,13},{1... | collective-permute-start | bytes 1179656 | tf_op jit(solution)/shard_map/ppermute | solution.py:43
  19.7 2.7 %collective-permute-start.14 = (bf16[2,64,1536]{2,1,0:T(8,128)(2,1)S(1)}, bf16[2,64,1536]{2,1,0:T(8,128)(2,1)S(1)}, u32[]{:S(2)}, u32[]{:S(2)}) collective-permute-start(bf16[2,64,1536]{2,1,0:T(8,128)(2,1)S(1)} %pad_maximum_fusion.refs_0_), channel_id=1, source_target_pairs={{0,8},{1,9},{2,10},{3,11},{4,12},{5,13},{6,14},{7,15},{8,0},{9,1},... | collective-permute-start | bytes 1179656 | tf_op jit(solution)/shard_map/ppermute | solution.py:43
  22.4 1.7 %collective-permute-done.refs_1_ = bf16[128,3072]{1,0:T(8,128)(2,1)S(1)} collective-permute-done((bf16[128,3072]{1,0:T(8,128)(2,1)S(1)}, bf16[128,3072]{1,0:T(8,128)(2,1)S(1)}, u32[]{:S(2)}, u32[]{:S(2)}) %collective-permute-start) | collective-permute-done | bytes 786464 | tf_op jit(solution)/shard_map/ppermute | solution.py:33
  24.1 2.8 %collective-permute-start.15 = (bf16[2,64,1536]{2,1,0:T(8,128)(2,1)S(1)}, bf16[2,64,1536]{2,1,0:T(8,128)(2,1)S(1)}, u32[]{:S(2)}, u32[]{:S(2)}) collective-permute-start(bf16[2,64,1536]{2,1,0:T(8,128)(2,1)S(1)} %pad_maximum_fusion.refs_0_), channel_id=1, source_target_pairs={{0,12},{1,13},{2,14},{3,15},{4,0},{5,1},{6,2},{7,3},{8,4},{9,5},{1... | collective-permute-start | bytes 1179656 | tf_op jit(solution)/shard_map/ppermute | solution.py:43
  26.9 6.7 %collective-permute-done.2.refs_3_.refs_4_ = bf16[128,3072]{1,0:T(8,128)(2,1)S(1)} collective-permute-done((bf16[128,3072]{1,0:T(8,128)(2,1)S(1)}, bf16[128,3072]{1,0:T(8,128)(2,1)S(1)}, u32[]{:S(2)}, u32[]{:S(2)}) %collective-permute-start.2) | collective-permute-done | bytes 786464 | tf_op jit(solution)/shard_map/ppermute | solution.py:33
  37.7 2.6 %transposed_tokens.1.mine_ref = bf16[1536,512]{1,0:T(8,128)(2,1)S(1)} custom-call(bf16[2,64,1536]{2,1,0:T(8,128)(2,1)S(1)} %pad_maximum_fusion.refs_0_, bf16[2,64,1536]{2,1,0:T(8,128)(2,1)S(1)} %collective-permute-done.13.refs_1_, bf16[2,64,1536]{2,1,0:T(8,128)(2,1)S(1)} %collective-permute-done.14.refs_2_, ...), custom_call_target="tpu_custom_call" | custom-call | bytes 6291456 | tf_op jit(solution)/shard_map/transposed_tokens/pallas_call | solution.py:102
  40.4 3.7 %copy-done.2 = bf16[1536,3072]{1,0:T(8,128)(2,1)S(1)} copy-done((bf16[1536,3072]{1,0:T(8,128)(2,1)S(1)}, bf16[1536,3072]{1,0:T(8,128)(2,1)}, u32[]{:S(2)}) %copy-start.2) | copy-done | bytes 9437208
  44.7 5.9 %input_part.3 = (f32[4,64,1536]{2,1,0:T(8,128)S(1)}, bf16[4,64,1536]{2,1,0:T(8,128)(2,1)S(1)}) custom-call(bf16[128,3072]{1,0:T(8,128)(2,1)S(1)} %hidden_gradient.1.refs_0_, bf16[128,3072]{1,0:T(8,128)(2,1)S(1)} %collective-permute-done.refs_1_, bf16[128,3072]{1,0:T(8,128)(2,1)S(1)} %collective-permute-done.1.refs_2_.refs_3_, ...), custom_call_target="tpu_custom_call" | custom-call | flops 4831838208 | bytes 12582912 | tf_op jit(solution)/shard_map/input_part/pallas_call | solution.py:212
  51.3 2.2 %collective-permute-done.4.refs_0_.refs_2_ = bf16[128,3072]{1,0:T(8,128)(2,1)S(1)} collective-permute-done((bf16[128,3072]{1,0:T(8,128)(2,1)S(1)}, bf16[128,3072]{1,0:T(8,128)(2,1)S(1)}, u32[]{:S(2)}, u32[]{:S(2)}) %collective-permute-start.4) | collective-permute-done | bytes 786464 | tf_op jit(solution)/shard_map/ppermute | solution.py:33
  53.4 4.5 %input_part.4 = (f32[3,64,1536]{2,1,0:T(8,128)S(1)}, bf16[3,64,1536]{2,1,0:T(8,128)(2,1)S(1)}) custom-call(bf16[128,3072]{1,0:T(8,128)(2,1)S(1)} %collective-permute-done.4.refs_0_.refs_2_, bf16[128,3072]{1,0:T(8,128)(2,1)S(1)} %collective-permute-done.5.refs_1_.refs_5_, bf16[128,3072]{1,0:T(8,128)(2,1)S(1)} %collective-permute-done.6.refs_2_.refs_8_, ...), custom_call_target="tpu_custom_call" | custom-call | flops 3623878656 | bytes 11796480 | tf_op jit(solution)/shard_map/input_part/pallas_call | solution.py:212
  58.3 3.2 %collective-permute-start.17 = (bf16[64,3072]{1,0:T(8,128)(2,1)S(1)}, bf16[64,3072]{1,0:T(8,128)(2,1)S(1)}, u32[]{:S(2)}, u32[]{:S(2)}) collective-permute-start(bf16[64,3072]{1,0:T(8,128)(2,1)S(1)} %slice.9), channel_id=1, source_target_pairs={{0,96},{16,112},{32,0},{48,16},{64,32},{80,48},{96,64},{112,80},{1... | collective-permute-start | bytes 1179656 | tf_op jit(solution)/shard_map/ppermute | solution.py:33
  63.6 2.8 %collective-permute-start.10 = (bf16[64,1536]{1,0:T(8,128)(2,1)}, bf16[64,1536]{1,0:T(8,128)(2,1)}, u32[]{:S(2)}, u32[]{:S(2)}) collective-permute-start(bf16[64,1536]{1,0:T(8,128)(2,1)} %get-tuple-element.35), channel_id=1, source_target_pairs={{0,12},{1,13},{2,14},{3,15},{4,0},{5,1},{6,2},{7,3},{8,4},{9,5},{1... | collective-permute-start | bytes 589832 | tf_op jit(solution)/shard_map/ppermute | solution.py:43
  71.2 4.5 %input_part.5 = (f32[1,64,1536]{2,1,0:T(8,128)S(1)}, bf16[1,64,1536]{2,1,0:T(8,128)(2,1)}) custom-call(bf16[64,3072]{1,0:T(8,128)(2,1)S(1)} %collective-permute-done.11.refs_0_.refs_6_, bf16[64,3072]{1,0:T(8,128)(2,1)S(1)} %collective-permute-done.17.refs_1_.refs_7_, bf16[1536,3072]{1,0:T(8,128)(2,1)S(1)} %held_weight.1.refs_4_.refs_3_.refs_2_), custom_call_target="tpu_custom_call" | custom-call | flops 1207959552 | bytes 10223616 | tf_op jit(solution)/shard_map/input_part/pallas_call | solution.py:212
  76.5 3.0 %held_rows.1.held = bf16[1024,3072]{1,0:T(8,128)(2,1)S(1)} custom-call(bf16[128,3072]{1,0:T(8,128)(2,1)} %copy-done.5, bf16[128,3072]{1,0:T(8,128)(2,1)} %copy-done.12, bf16[128,3072]{1,0:T(8,128)(2,1)} %copy-done.15, bf16[128,3072]{1,0:T(8,128)(2,1)} %copy-done.14, bf16[128,3072]{1,0:T(8,128)(2,1)} %copy-done.13, bf16[128,3072]{1,0:T(8,128)(2,1)} %copy-done.6, ...), custom_call_target="tpu_custom_call" | custom-call | bytes 12582912 | tf_op jit(solution)/shard_map/held_rows/pallas_call | solution.py:295
  79.6 1.5 %dealt.3 = (f32[64,1536]{1,0:T(8,128)S(1)}, bf16[64,1536]{1,0:T(8,128)(2,1)S(1)}, bf16[64,1536]{1,0:T(8,128)(2,1)S(1)}, bf16[64,1536]{1,0:T(8,128)(2,1)S(1)}) custom-call(f32[4,64,1536]{2,1,0:T(8,128)S(1)} %get-tuple-element.26.refs_0_.refs_2_.refs_6_, bf16[4,64,1536]{2,1,0:T(8,128)(2,1)S(1)} %collective-permute-done.3.refs_1_.refs_3_.refs_7_, ...), custom_call_target="tpu_custom_call" | custom-call | bytes 3932160 | tf_op jit(solution)/shard_map/dealt/pallas_call | solution.py:251
  81.1 1.9 %collective-permute-start.19 = (bf16[64,1536]{1,0:T(8,128)(2,1)S(1)}, bf16[64,1536]{1,0:T(8,128)(2,1)S(1)}, u32[]{:S(2)}, u32[]{:S(2)}) collective-permute-start(bf16[64,1536]{1,0:T(8,128)(2,1)S(1)} %get-tuple-element.41), channel_id=1, source_target_pairs={{0,4},{1,5},{2,6},{3,7},{4,8},{5,9},{6,10},{7,11},{8,12},{9,13},{1... | collective-permute-start | bytes 589832 | tf_op jit(solution)/shard_map/ppermute | solution.py:43
  82.9 1.4 %collective-permute-start.21 = (bf16[64,1536]{1,0:T(8,128)(2,1)S(1)}, bf16[64,1536]{1,0:T(8,128)(2,1)S(1)}, u32[]{:S(2)}, u32[]{:S(2)}) collective-permute-start(bf16[64,1536]{1,0:T(8,128)(2,1)S(1)} %get-tuple-element.46), channel_id=1, source_target_pairs={{0,12},{1,13},{2,14},{3,15},{4,0},{5,1},{6,2},{7,3},{8,4},{9,5},{1... | collective-permute-start | bytes 589832 | tf_op jit(solution)/shard_map/ppermute | solution.py:43
  84.4 1.5 %collective-permute-start.20 = (bf16[64,1536]{1,0:T(8,128)(2,1)S(1)}, bf16[64,1536]{1,0:T(8,128)(2,1)S(1)}, u32[]{:S(2)}, u32[]{:S(2)}) collective-permute-start(bf16[64,1536]{1,0:T(8,128)(2,1)S(1)} %get-tuple-element.45), channel_id=1, source_target_pairs={{0,8},{1,9},{2,10},{3,11},{4,12},{5,13},{6,14},{7,15},{8,0},{9,1},... | collective-permute-start | bytes 589832 | tf_op jit(solution)/shard_map/ppermute | solution.py:43
  85.9 8.4 %weight_gradient.2.refs_0_ = bf16[1536,3072]{1,0:T(8,128)(2,1)} custom-call(bf16[1536,1024]{1,0:T(8,128)(2,1)S(1)} %copy-done.1, bf16[1024,3072]{1,0:T(8,128)(2,1)S(1)} %held_rows.1.held), custom_call_target="tpu_custom_call" | custom-call | flops 9663676416 | bytes 6291456 | tf_op jit(solution)/shard_map/weight_gradient/pallas_call | solution.py:323
  97.1 4.8 %weight_gradient.3 = bf16[1536,3072]{1,0:T(8,128)(2,1)} custom-call(bf16[1536,1024]{1,0:T(8,128)(2,1)S(1)} %copy-done.1, bf16[1024,3072]{1,0:T(8,128)(2,1)S(1)} %held_rows.1.held, bf16[1536,3072]{1,0:T(8,128)(2,1)} %weight_gradient.2.refs_0_), custom_call_target="tpu_custom_call", output_to_operand_aliasing={{}: (2, {})} | custom-call | flops 4831838208 | bytes 3145728 | tf_op jit(solution)/shard_map/weight_gradient/pallas_call | solution.py:323
  101.9 2.0 %collective-permute-done.22 = bf16[64,1536]{1,0:T(8,128)(2,1)S(1)} collective-permute-done((bf16[64,1536]{1,0:T(8,128)(2,1)S(1)}, bf16[64,1536]{1,0:T(8,128)(2,1)S(1)}, u32[]{:S(2)}, u32[]{:S(2)}) %collective-permute-start.22) | collective-permute-done | bytes 196640 | tf_op jit(solution)/shard_map/ppermute | solution.py:43
  (83 shorter events, 22.4 us)
Async XLA Ops:
  4.2 40.5 %copy-start.5 = (bf16[128,3072]{1,0:T(8,128)(2,1)}, bf16[128,3072]{1,0:T(8,128)(2,1)S(1)}, u32[]{:S(2)}) copy-start(bf16[128,3072]{1,0:T(8,128)(2,1)S(1)} %hidden_gradient.1.refs_0_) | copy-start | bytes 2359300
  4.2 20.0 %collective-permute-start = (bf16[128,3072]{1,0:T(8,128)(2,1)S(1)}, bf16[128,3072]{1,0:T(8,128)(2,1)S(1)}, u32[]{:S(2)}, u32[]{:S(2)}) collective-permute-start(bf16[128,3072]{1,0:T(8,128)(2,1)S(1)} %hidden_gradient.1.refs_0_), channel_id=1, source_target_pairs={{0,96},{16,112},{32,0},{48,16},{64,32},{80,48},{96,64},{112,80},{1... | collective-permute-start | bytes 2359304 | tf_op jit(solution)/shard_map/ppermute | solution.py:33
  7.3 9.9 %collective-permute-start.12 = (bf16[64,1536]{1,0:T(8,128)(2,1)}, bf16[64,1536]{1,0:T(8,128)(2,1)S(1)}, u32[]{:S(2)}, u32[]{:S(2)}) collective-permute-start(bf16[64,1536]{1,0:T(8,128)(2,1)} %param.4), channel_id=1, source_target_pairs={{0,2},{1,3},{2,0},{3,1},{4,6},{5,7},{6,4},{7,5},{8,10},{9,11},{10,... | collective-permute-start | bytes 589832 | tf_op jit(solution)/shard_map/ppermute | solution.py:43
  11.2 22.4 %collective-permute-start.2 = (bf16[128,3072]{1,0:T(8,128)(2,1)S(1)}, bf16[128,3072]{1,0:T(8,128)(2,1)S(1)}, u32[]{:S(2)}, u32[]{:S(2)}) collective-permute-start(bf16[128,3072]{1,0:T(8,128)(2,1)S(1)} %hidden_gradient.1.refs_0_), channel_id=1, source_target_pairs={{0,16},{16,0},{32,48},{48,32},{64,80},{80,64},{96,112},{112,96},{1... | collective-permute-start | bytes 2359304 | tf_op jit(solution)/shard_map/ppermute | solution.py:33
  12.2 22.1 %collective-permute-start.1 = (bf16[128,3072]{1,0:T(8,128)(2,1)S(1)}, bf16[128,3072]{1,0:T(8,128)(2,1)S(1)}, u32[]{:S(2)}, u32[]{:S(2)}) collective-permute-start(bf16[128,3072]{1,0:T(8,128)(2,1)S(1)} %hidden_gradient.1.refs_0_), channel_id=1, source_target_pairs={{0,32},{16,48},{32,64},{48,80},{64,96},{80,112},{96,0},{112,16},{1... | collective-permute-start | bytes 2359304 | tf_op jit(solution)/shard_map/ppermute | solution.py:33
  18.2 17.5 %collective-permute-start.13 = (bf16[2,64,1536]{2,1,0:T(8,128)(2,1)S(1)}, bf16[2,64,1536]{2,1,0:T(8,128)(2,1)S(1)}, u32[]{:S(2)}, u32[]{:S(2)}) collective-permute-start(bf16[2,64,1536]{2,1,0:T(8,128)(2,1)S(1)} %pad_maximum_fusion.refs_0_), channel_id=1, source_target_pairs={{0,4},{1,5},{2,6},{3,7},{4,8},{5,9},{6,10},{7,11},{8,12},{9,13},{1... | collective-permute-start | bytes 1179656 | tf_op jit(solution)/shard_map/ppermute | solution.py:43
  19.7 18.0 %collective-permute-start.14 = (bf16[2,64,1536]{2,1,0:T(8,128)(2,1)S(1)}, bf16[2,64,1536]{2,1,0:T(8,128)(2,1)S(1)}, u32[]{:S(2)}, u32[]{:S(2)}) collective-permute-start(bf16[2,64,1536]{2,1,0:T(8,128)(2,1)S(1)} %pad_maximum_fusion.refs_0_), channel_id=1, source_target_pairs={{0,8},{1,9},{2,10},{3,11},{4,12},{5,13},{6,14},{7,15},{8,0},{9,1},... | collective-permute-start | bytes 1179656 | tf_op jit(solution)/shard_map/ppermute | solution.py:43
  24.1 13.5 %collective-permute-start.15 = (bf16[2,64,1536]{2,1,0:T(8,128)(2,1)S(1)}, bf16[2,64,1536]{2,1,0:T(8,128)(2,1)S(1)}, u32[]{:S(2)}, u32[]{:S(2)}) collective-permute-start(bf16[2,64,1536]{2,1,0:T(8,128)(2,1)S(1)} %pad_maximum_fusion.refs_0_), channel_id=1, source_target_pairs={{0,12},{1,13},{2,14},{3,15},{4,0},{5,1},{6,2},{7,3},{8,4},{9,5},{1... | collective-permute-start | bytes 1179656 | tf_op jit(solution)/shard_map/ppermute | solution.py:43
  33.6 19.8 %collective-permute-start.5 = (bf16[128,3072]{1,0:T(8,128)(2,1)S(1)}, bf16[128,3072]{1,0:T(8,128)(2,1)S(1)}, u32[]{:S(2)}, u32[]{:S(2)}) collective-permute-start(bf16[128,3072]{1,0:T(8,128)(2,1)S(1)} %collective-permute-done.2.refs_3_.refs_4_), channel_id=1, source_target_pairs={{0,96},{16,112},{32,0},{48,16},{64,32},{80,48},{96,64},{112,80},{1... | collective-permute-start | bytes 2359304 | tf_op jit(solution)/shard_map/ppermute | solution.py:33
  34.4 19.0 %collective-permute-start.4 = (bf16[128,3072]{1,0:T(8,128)(2,1)S(1)}, bf16[128,3072]{1,0:T(8,128)(2,1)S(1)}, u32[]{:S(2)}, u32[]{:S(2)}) collective-permute-start(bf16[128,3072]{1,0:T(8,128)(2,1)S(1)} %collective-permute-done.1.refs_2_.refs_3_), channel_id=1, source_target_pairs={{0,32},{16,48},{32,64},{48,80},{64,96},{80,112},{96,0},{112,16},{1... | collective-permute-start | bytes 2359304 | tf_op jit(solution)/shard_map/ppermute | solution.py:33
  35.7 17.7 %collective-permute-start.6 = (bf16[128,3072]{1,0:T(8,128)(2,1)S(1)}, bf16[128,3072]{1,0:T(8,128)(2,1)S(1)}, u32[]{:S(2)}, u32[]{:S(2)}) collective-permute-start(bf16[128,3072]{1,0:T(8,128)(2,1)S(1)} %collective-permute-done.1.refs_2_.refs_3_), channel_id=1, source_target_pairs={{0,16},{16,0},{32,48},{48,32},{64,80},{80,64},{96,112},{112,96},{1... | collective-permute-start | bytes 2359304 | tf_op jit(solution)/shard_map/ppermute | solution.py:33
  40.3 26.9 %collective-permute-start.16 = (bf16[1536,512]{1,0:T(8,128)(2,1)S(1)}, bf16[1536,512]{1,0:T(8,128)(2,1)S(1)}, u32[]{:S(2)}, u32[]{:S(2)}) collective-permute-start(bf16[1536,512]{1,0:T(8,128)(2,1)S(1)} %transposed_tokens.1.mine_ref), channel_id=1, source_target_pairs={{0,1},{1,0},{2,3},{3,2},{4,5},{5,4},{6,7},{7,6},{8,9},{9,8},{10,11... | collective-permute-start | bytes 4718600 | tf_op jit(solution)/shard_map/ppermute | solution.py:43
  50.6 10.9 %collective-permute-start.3 = (bf16[4,64,1536]{2,1,0:T(8,128)(2,1)S(1)}, bf16[4,64,1536]{2,1,0:T(8,128)(2,1)S(1)}, u32[]{:S(2)}, u32[]{:S(2)}) collective-permute-start(bf16[4,64,1536]{2,1,0:T(8,128)(2,1)S(1)} %get-tuple-element.27), channel_id=1, source_target_pairs={{0,1},{1,0},{2,3},{3,2},{4,5},{5,4},{6,7},{7,6},{8,9},{9,8},{10,11... | collective-permute-start | bytes 2359304 | tf_op jit(solution)/shard_map/ppermute | solution.py:43
  58.0 3.6 %collective-permute-start.7 = (bf16[3,64,1536]{2,1,0:T(8,128)(2,1)S(1)}, bf16[3,64,1536]{2,1,0:T(8,128)(2,1)S(1)}, u32[]{:S(2)}, u32[]{:S(2)}) collective-permute-start(bf16[3,64,1536]{2,1,0:T(8,128)(2,1)S(1)} %get-tuple-element.31), channel_id=1, source_target_pairs={{0,1},{1,0},{2,3},{3,2},{4,5},{5,4},{6,7},{7,6},{8,9},{9,8},{10,11... | collective-permute-start | bytes 1769480 | tf_op jit(solution)/shard_map/ppermute | solution.py:43
  58.1 13.0 %collective-permute-start.11 = (bf16[64,3072]{1,0:T(8,128)(2,1)S(1)}, bf16[64,3072]{1,0:T(8,128)(2,1)S(1)}, u32[]{:S(2)}, u32[]{:S(2)}) collective-permute-start(bf16[64,3072]{1,0:T(8,128)(2,1)S(1)} %slice.8), channel_id=1, source_target_pairs={{0,32},{16,48},{32,64},{48,80},{64,96},{80,112},{96,0},{112,16},{1... | collective-permute-start | bytes 1179656 | tf_op jit(solution)/shard_map/ppermute | solution.py:33
  58.3 12.8 %collective-permute-start.17 = (bf16[64,3072]{1,0:T(8,128)(2,1)S(1)}, bf16[64,3072]{1,0:T(8,128)(2,1)S(1)}, u32[]{:S(2)}, u32[]{:S(2)}) collective-permute-start(bf16[64,3072]{1,0:T(8,128)(2,1)S(1)} %slice.9), channel_id=1, source_target_pairs={{0,96},{16,112},{32,0},{48,16},{64,32},{80,48},{96,64},{112,80},{1... | collective-permute-start | bytes 1179656 | tf_op jit(solution)/shard_map/ppermute | solution.py:33
  63.6 15.9 %collective-permute-start.10 = (bf16[64,1536]{1,0:T(8,128)(2,1)}, bf16[64,1536]{1,0:T(8,128)(2,1)}, u32[]{:S(2)}, u32[]{:S(2)}) collective-permute-start(bf16[64,1536]{1,0:T(8,128)(2,1)} %get-tuple-element.35), channel_id=1, source_target_pairs={{0,12},{1,13},{2,14},{3,15},{4,0},{5,1},{6,2},{7,3},{8,4},{9,5},{1... | collective-permute-start | bytes 589832 | tf_op jit(solution)/shard_map/ppermute | solution.py:43
  66.4 13.2 %collective-permute-start.9 = (bf16[64,1536]{1,0:T(8,128)(2,1)}, bf16[64,1536]{1,0:T(8,128)(2,1)}, u32[]{:S(2)}, u32[]{:S(2)}) collective-permute-start(bf16[64,1536]{1,0:T(8,128)(2,1)} %get-tuple-element.34), channel_id=1, source_target_pairs={{0,8},{1,9},{2,10},{3,11},{4,12},{5,13},{6,14},{7,15},{8,0},{9,1},... | collective-permute-start | bytes 589832 | tf_op jit(solution)/shard_map/ppermute | solution.py:43
  68.3 11.3 %collective-permute-start.8 = (bf16[64,1536]{1,0:T(8,128)(2,1)}, bf16[64,1536]{1,0:T(8,128)(2,1)}, u32[]{:S(2)}, u32[]{:S(2)}) collective-permute-start(bf16[64,1536]{1,0:T(8,128)(2,1)} %get-tuple-element.33), channel_id=1, source_target_pairs={{0,4},{1,5},{2,6},{3,7},{4,8},{5,9},{6,10},{7,11},{8,12},{9,13},{1... | collective-permute-start | bytes 589832 | tf_op jit(solution)/shard_map/ppermute | solution.py:43
  76.4 3.1 %collective-permute-start.18 = (bf16[1,64,1536]{2,1,0:T(8,128)(2,1)}, bf16[1,64,1536]{2,1,0:T(8,128)(2,1)}, u32[]{:S(2)}, u32[]{:S(2)}) collective-permute-start(bf16[1,64,1536]{2,1,0:T(8,128)(2,1)} %get-tuple-element.38), channel_id=1, source_target_pairs={{0,1},{1,0},{2,3},{3,2},{4,5},{5,4},{6,7},{7,6},{8,9},{9,8},{10,11... | collective-permute-start | bytes 589832 | tf_op jit(solution)/shard_map/ppermute | solution.py:43
  81.1 13.4 %collective-permute-start.19 = (bf16[64,1536]{1,0:T(8,128)(2,1)S(1)}, bf16[64,1536]{1,0:T(8,128)(2,1)S(1)}, u32[]{:S(2)}, u32[]{:S(2)}) collective-permute-start(bf16[64,1536]{1,0:T(8,128)(2,1)S(1)} %get-tuple-element.41), channel_id=1, source_target_pairs={{0,4},{1,5},{2,6},{3,7},{4,8},{5,9},{6,10},{7,11},{8,12},{9,13},{1... | collective-permute-start | bytes 589832 | tf_op jit(solution)/shard_map/ppermute | solution.py:43
  82.9 11.4 %collective-permute-start.21 = (bf16[64,1536]{1,0:T(8,128)(2,1)S(1)}, bf16[64,1536]{1,0:T(8,128)(2,1)S(1)}, u32[]{:S(2)}, u32[]{:S(2)}) collective-permute-start(bf16[64,1536]{1,0:T(8,128)(2,1)S(1)} %get-tuple-element.46), channel_id=1, source_target_pairs={{0,12},{1,13},{2,14},{3,15},{4,0},{5,1},{6,2},{7,3},{8,4},{9,5},{1... | collective-permute-start | bytes 589832 | tf_op jit(solution)/shard_map/ppermute | solution.py:43
  84.4 10.1 %collective-permute-start.20 = (bf16[64,1536]{1,0:T(8,128)(2,1)S(1)}, bf16[64,1536]{1,0:T(8,128)(2,1)S(1)}, u32[]{:S(2)}, u32[]{:S(2)}) collective-permute-start(bf16[64,1536]{1,0:T(8,128)(2,1)S(1)} %get-tuple-element.45), channel_id=1, source_target_pairs={{0,8},{1,9},{2,10},{3,11},{4,12},{5,13},{6,14},{7,15},{8,0},{9,1},... | collective-permute-start | bytes 589832 | tf_op jit(solution)/shard_map/ppermute | solution.py:43
  95.8 8.1 %collective-permute-start.22 = (bf16[64,1536]{1,0:T(8,128)(2,1)S(1)}, bf16[64,1536]{1,0:T(8,128)(2,1)S(1)}, u32[]{:S(2)}, u32[]{:S(2)}) collective-permute-start(bf16[64,1536]{1,0:T(8,128)(2,1)S(1)} %get-tuple-element.48), channel_id=1, source_target_pairs={{0,2},{1,3},{2,0},{3,1},{4,6},{5,7},{6,4},{7,5},{8,10},{9,11},{10,... | collective-permute-start | bytes 589832 | tf_op jit(solution)/shard_map/ppermute | solution.py:43
  (21 other events, 113.6 us)
